TPU v7x, 32 devices: a whole 2x2x4 slice. The times are simulated.
32 devices in a mesh: groups: 2 (over y), cells: 4 (over z), tm: 4 (over x, core).
Axes of the slice: x: 2, y: 2, z: 4, core: 2. Of those that a mesh axis runs over, the one named last changes fastest.
Arguments:
- observed: float32 [1024, 16384], P('tm', ('groups', 'cells')), parts along dimension 1
- mask: int32 [1024, 16384], P('tm', ('groups', 'cells')), parts along dimension 1, may hold values 0 or 1
- noise: float32 [16384], P(('groups', 'cells')), parts along dimension 0, may hold values from 0.05 to 0.5
- spread: float32 [16384], P(('groups', 'cells')), parts along dimension 0, may hold values from 0.5 to 1
- taps: float32 [32], replicated, may hold values from 0.1 to 1
- neighbours: int32 [8, 16384], P(None, ('groups', 'cells')), parts along dimension 1, may hold values from 0 to 8191, as said below
- regions: int32 [16384], P(('groups', 'cells')), parts along dimension 0, may hold values from 0 to 31, never falling along the last dimension, each value on 1 to 512 neighbouring positions
Outputs:
- solution: float32 [1024, 16384], P('tm', ('groups', 'cells')), parts along dimension 1
- residual: float32 [1024, 16384], P('tm', ('groups', 'cells')), parts along dimension 1
There are 2 independent parts, one for each index of `groups`. A program takes and returns all parts, laid end to end along the dimension named above; an argument that names none is the same for every part. Nothing has to cross between parts.
Inputs may be any that keep to these rules, and one draw needn't show every extreme that they name: For every slot p and cell c, neighbours[p, c] = e implies neighbours[p, e] = c, and |e - c| < 32. `regions`: region ids never fall from one cell to the next.
All inputs are finite; a program needn't handle non-finite values. No bound on the sum of `mask` on one device may be relied on, other than what follows from the above.
Results may differ from a plain program's by a relative error of at most 0.0003.
Values sent between devices are 32-bit elements; how exact they have to be, the bound alone decides.
A program may use at most 192 MiB of HBM per device.

v0:
```python
import jax
import jax.numpy as jnp
from jax import lax
from jax.sharding import PartitionSpec as P

W = 32
HB = 32
ITERS = 3


pair_scale = 0.075
temporal_diag = 2.0
tap_total = 0.9


def extended(cells, sides, width, closed):
    for axis, dim in sides:
        count = lax.axis_size(axis)
        ends = count if closed else count - 1
        head = lax.slice_in_dim(cells, 0, width, axis=dim)
        tail = lax.slice_in_dim(cells, cells.shape[dim] - width, cells.shape[dim], axis=dim)
        cells = jnp.concatenate(
            [
                lax.ppermute(tail, axis, [(i, (i + 1) % count) for i in range(ends)]),
                cells,
                lax.ppermute(head, axis, [((i + 1) % count, i) for i in range(ends)]),
            ],
            axis=dim,
        )
    return cells


def squares(residual):
    return lax.psum(jnp.sum(residual * residual), ("cells", "tm"))


def on_device(observed, mask, noise, spread, taps, neighbours, regions):
    coefs = taps * (tap_total / W)
    tile_cells = observed.shape[1]
    mask_local = mask.astype(jnp.float32)
    anchor = lax.axis_index("cells") * tile_cells
    region_padded = extended(regions, (("cells", 0),), HB, False)
    local_index = neighbours - anchor + HB
    region_pair = jnp.take(region_padded, local_index)
    pair_weight = (
        pair_scale * spread[None, :] * (region_pair == regions[None, :]).astype(jnp.float32)
    )
    width_local = spread.shape[0]
    block_cells = 128
    block_count = width_local // block_cells
    window_cells = block_cells + 2 * HB
    block_starts = jnp.arange(width_local, dtype=jnp.int32) // block_cells * block_cells
    offsets_in = (local_index - block_starts[None, :]).reshape(
        neighbours.shape[0], block_count, 1, block_cells
    )
    weights_in = pair_weight.reshape(neighbours.shape[0], block_count, 1, block_cells)
    span_ids = jnp.arange(window_cells, dtype=jnp.int32)[None, :, None]
    centre_ids = (jnp.arange(block_cells, dtype=jnp.int32) + HB)[None, None, :]
    band = (span_ids == centre_ids).astype(jnp.float32) * (1.0 / spread).reshape(
        block_count, 1, block_cells
    )
    for slot in range(neighbours.shape[0]):
        band = band + (span_ids == offsets_in[slot]).astype(jnp.float32) * weights_in[slot]
    right = mask_local * observed
    solution = jnp.zeros_like(right)
    residual = right
    direction = right
    norm_now = squares(residual)
    for count in range(ITERS):
        masked = mask_local * direction
        scaled = spread[None, :] * masked
        length = direction.shape[0]
        padded = extended(scaled, (("cells", 1),), HB, False)
        start = HB - HB
        windows = jnp.stack(
            [
                padded[:, start + index * block_cells : start + index * block_cells + window_cells]
                for index in range(block_count)
            ],
            1,
        )
        result = jnp.einsum("tbj,bji->tbi", windows, band, precision=lax.Precision.HIGHEST)
        mixed = result.reshape(padded.shape[0], width_local)
        beside_all = extended(mixed, (("tm", 0),), W, True)
        smooth = temporal_diag * beside_all[W : W + length]
        for offset in range(1, W + 1):
            smooth = smooth + coefs[offset - 1] * (
                beside_all[W - offset : W - offset + length]
                + beside_all[W + offset : W + offset + length]
            )
        image = noise[None, :] * direction + mask_local * smooth
        alpha = norm_now / lax.psum(jnp.sum(direction * image), ("cells", "tm"))
        solution = solution + alpha * direction
        residual = residual - alpha * image
        if count + 1 < ITERS:
            norm_next = squares(residual)
            direction = residual + norm_next / norm_now * direction
            norm_now = norm_next
    return (solution, residual)


def solution(mesh):
    return jax.shard_map(
        on_device,
        mesh=mesh,
        in_specs=(
            P("tm", ("groups", "cells")),
            P("tm", ("groups", "cells")),
            P(("groups", "cells")),
            P(("groups", "cells")),
            P(),
            P(None, ("groups", "cells")),
            P(("groups", "cells")),
        ),
        out_specs=(P("tm", ("groups", "cells")), P("tm", ("groups", "cells"))),
        check_vma=False,
    )
```

profile of v0, /device:TPU:0, one launch (start us, length us, event | category | flops | bytes accessed | tf_op | source)
XLA Modules:
  0.0 798.9 jit_solution(18114101031650001298)
XLA Ops:
  2.7 5.6 collective-permute-start
  10.2 2.9 copy.18
  13.1 3.3 multiply_multiply_fusion.2
  19.0 4.6 collective-permute-start.2
  23.9 90.5 %gather_fusion = s32[16384]{0:T(1024)S(1)} fusion(s32[2112]{0:T(1024)S(1)} %concatenate.231, s32[16384]{0:T(1024)S(1)} %broadcast_clamp_fusion), kind=kCustom, calls=%fused_computation | custom fusion | bytes 196608 | tf_op jit(solution)/shard_map/jit(_take)/gather | solution.py:44
  116.7 5.2 fusion.543
  123.6 2.3 copy.19
  128.9 6.4 collective-permute-done.4
  136.7 2.3 copy.22
  138.9 138.6 %multiply_reduce_fusion.4 = (f32[]{:T(128)}, f32[]{:T(128)}, f32[256,2048]{0,1:T(8,128)}) fusion(f32[256,2048]{0,1:T(8,128)} %get-tuple-element.24, f32[32,2048]{0,1:T(8,128)} %copy.22, f32[256,2048]{0,1:T(8,128)} %bitcast.266, f32[32,2048]{0,1:T(8,128)S(1)} %copy.20, f32[]{:T(128)} %bitcast.69, f32[]{:T(128)} %bitcast.68, f32[]{:T(128)} %bitcast.67, ...), kind=kLoop, calls=%fused_computation.871 | loop fusion | flops 88604672 | bytes 8921224 | tf_op jit(solution)/shard_map/reduce_sum | solution.py:92
  277.5 30.2 %all-reduce = (f32[]{:T(128)}, f32[]{:T(128)}) all-reduce(f32[]{:T(128)} %get-tuple-element.9, f32[]{:T(128)} %get-tuple-element.8), channel_id=1, replica_groups=mesh['groups'=2,'cells'=4,'tm'=4] {'cells','tm'}, use_global_device_ids=true, to_apply=%region_1.2 | all-reduce | flops 2 | bytes 16 | tf_op jit(solution)/shard_map/psum | solution.py:34
  309.0 3.4 multiply_reduce_fusion.3
  312.4 30.1 %psum.44 = f32[]{:T(128)} all-reduce(f32[]{:T(128)} %multiply_reduce_fusion.3), channel_id=1, replica_groups=mesh['groups'=2,'cells'=4,'tm'=4] {'cells','tm'}, use_global_device_ids=true, to_apply=%region_5.6 | all-reduce | flops 1 | bytes 8 | tf_op jit(solution)/shard_map/psum | solution.py:34
  343.8 4.0 multiply_multiply_fusion.1
  351.2 3.8 collective-permute-done.7
  355.1 5.2 fusion.542
  364.5 2.2 collective-permute-start.9
  366.7 5.0 collective-permute-done.8
  373.0 2.3 copy.26
  375.2 139.4 %multiply_reduce_fusion.2 = (f32[]{:T(128)}, f32[256,2048]{0,1:T(8,128)}) fusion(f32[256,2048]{0,1:T(8,128)} %get-tuple-element.21, f32[32,2048]{0,1:T(8,128)} %copy.26, f32[256,2048]{0,1:T(8,128)} %bitcast.268, f32[32,2048]{0,1:T(8,128)S(1)} %copy.24, f32[]{:T(128)} %bitcast.69, f32[]{:T(128)} %bitcast.68, f32[]{:T(128)} %bitcast.67, f32[]{:T(128)} %bitcast.66, ...), kind=kLoop, calls=%fused_computation.866 | loop fusion | flops 87556096 | bytes 8921220 | tf_op jit(solution)/shard_map/reduce_sum | solution.py:92
  514.7 30.2 %psum.45 = f32[]{:T(128)} all-reduce(f32[]{:T(128)} %get-tuple-element.18), channel_id=1, replica_groups=mesh['groups'=2,'cells'=4,'tm'=4] {'cells','tm'}, use_global_device_ids=true, to_apply=%region_7.8 | all-reduce | flops 1 | bytes 8 | tf_op jit(solution)/shard_map/psum | solution.py:92
  546.2 5.4 multiply_reduce_fusion.1
  551.5 30.1 %psum.46 = f32[]{:T(128)} all-reduce(f32[]{:T(128)} %get-tuple-element.16), channel_id=1, replica_groups=mesh['groups'=2,'cells'=4,'tm'=4] {'cells','tm'}, use_global_device_ids=true, to_apply=%region_9.10 | all-reduce | flops 1 | bytes 8 | tf_op jit(solution)/shard_map/psum | solution.py:34
  582.8 4.0 multiply_multiply_fusion
  590.1 3.8 collective-permute-done.11
  594.0 5.2 fusion.541
  605.3 5.5 collective-permute-done.12
  612.1 2.3 copy.30
  614.3 142.3 %multiply_reduce_fusion = (f32[]{:T(128)}, f32[256,2048]{0,1:T(8,128)}) fusion(f32[256,2048]{0,1:T(8,128)} %get-tuple-element.15, f32[32,2048]{0,1:T(8,128)} %copy.30, f32[256,2048]{0,1:T(8,128)} %bitcast.264, f32[32,2048]{0,1:T(8,128)S(1)} %copy.28, f32[]{:T(128)} %bitcast.69, f32[]{:T(128)} %bitcast.68, f32[]{:T(128)} %bitcast.67, f32[]{:T(128)} %bitcast.66, ...), kind=kLoop, calls=%fused_computation.861 | loop fusion | flops 87556096 | bytes 8921220 | tf_op jit(solution)/shard_map/reduce_sum | solution.py:92
  756.6 30.1 %psum.47 = f32[]{:T(128)} all-reduce(f32[]{:T(128)} %get-tuple-element.12), channel_id=1, replica_groups=mesh['groups'=2,'cells'=4,'tm'=4] {'cells','tm'}, use_global_device_ids=true, to_apply=%region_11.12 | all-reduce | flops 1 | bytes 8 | tf_op jit(solution)/shard_map/psum | solution.py:92
  787.9 6.1 multiply_subtract_fusion
  794.0 2.9 copy.32
  (196 shorter events, 35.8 us)
Async XLA Ops:
  1.4 22.4 %collective-permute-start.1 = (s32[32]{0:T(128)S(1)}, s32[32]{0:T(128)S(1)}, u32[]{:S(2)}, u32[]{:S(2)}) collective-permute-start(s32[32]{0:T(128)S(1)} %get-tuple-element.57), channel_id=1, source_target_pairs={{4,0},{8,4},{12,8},{5,1},{9,5},{13,9},{6,2},{10,6},{14,10},{7,3},{... | collective-permute-start | bytes 392 | tf_op jit(solution)/shard_map/ppermute | solution.py:26
  2.7 21.1 %collective-permute-start = (s32[32]{0:T(128)S(1)}, s32[32]{0:T(128)S(1)}, u32[]{:S(2)}, u32[]{:S(2)}) collective-permute-start(s32[32]{0:T(128)S(1)} %get-tuple-element.58), channel_id=1, source_target_pairs={{0,4},{4,8},{8,12},{1,5},{5,9},{9,13},{2,6},{6,10},{10,14},{3,7},{... | collective-permute-start | bytes 392 | tf_op jit(solution)/shard_map/ppermute | solution.py:24
  13.1 10.5 %copy-start.5 = (s32[8,2048]{1,0:T(8,128)S(1)}, s32[8,2048]{1,0:T(8,128)}, u32[]{:S(2)}) copy-start(s32[8,2048]{1,0:T(8,128)} %param.12) | copy-start | bytes 196612
  13.1 10.7 %copy-start.8 = (s32[2048]{0:T(1024)S(1)}, s32[2048]{0:T(1024)}, u32[]{:S(2)}) copy-start(s32[2048]{0:T(1024)} %param.13) | copy-start | bytes 24580
  17.7 98.8 %collective-permute-start.3 = (f32[256,32]{0,1:T(8,128)S(1)}, f32[256,32]{0,1:T(8,128)S(1)}, u32[]{:S(2)}, u32[]{:S(2)}) collective-permute-start(f32[256,32]{0,1:T(8,128)S(1)} %get-tuple-element.35), channel_id=1, source_target_pairs={{4,0},{8,4},{12,8},{5,1},{9,5},{13,9},{6,2},{10,6},{14,10},{7,3},{... | collective-permute-start | bytes 98312 | tf_op jit(solution)/shard_map/ppermute | solution.py:26
  19.0 95.7 %collective-permute-start.2 = (f32[256,32]{0,1:T(8,128)S(1)}, f32[256,32]{0,1:T(8,128)S(1)}, u32[]{:S(2)}, u32[]{:S(2)}) collective-permute-start(f32[256,32]{0,1:T(8,128)S(1)} %get-tuple-element.36), channel_id=1, source_target_pairs={{0,4},{4,8},{8,12},{1,5},{5,9},{9,13},{2,6},{6,10},{10,14},{3,7},{... | collective-permute-start | bytes 98312 | tf_op jit(solution)/shard_map/ppermute | solution.py:24
  23.7 92.9 %copy-start.9 = (s32[1,2048]{1,0:T(1,128)}, s32[1,2048]{1,0:T(1,128)S(1)}, u32[]{:S(2)}) copy-start(s32[1,2048]{1,0:T(1,128)S(1)} %get-tuple-element.41) | copy-start | bytes 24580
  23.7 92.9 %copy-start.12 = (s32[1,2048]{1,0:T(1,128)}, s32[1,2048]{1,0:T(1,128)S(1)}, u32[]{:S(2)}) copy-start(s32[1,2048]{1,0:T(1,128)S(1)} %get-tuple-element.42) | copy-start | bytes 24580
  23.7 92.9 %copy-start.15 = (s32[1,2048]{1,0:T(1,128)}, s32[1,2048]{1,0:T(1,128)S(1)}, u32[]{:S(2)}) copy-start(s32[1,2048]{1,0:T(1,128)S(1)} %get-tuple-element.43) | copy-start | bytes 24580
  23.7 92.9 %copy-start.18 = (s32[1,2048]{1,0:T(1,128)}, s32[1,2048]{1,0:T(1,128)S(1)}, u32[]{:S(2)}) copy-start(s32[1,2048]{1,0:T(1,128)S(1)} %get-tuple-element.44) | copy-start | bytes 24580
  23.8 92.8 %copy-start.21 = (f32[16,128]{1,0:T(8,128)}, f32[16,128]{1,0:T(8,128)S(1)}, u32[]{:S(2)}) copy-start(f32[16,128]{1,0:T(8,128)S(1)} %get-tuple-element.55) | copy-start | bytes 24580
  125.8 13.1 %copy-start.7 = (f32[2048]{0:T(1024)S(1)}, f32[2048]{0:T(1024)}, u32[]{:S(2)}) copy-start(f32[2048]{0:T(1024)} %param.9) | copy-start | bytes 24580
  126.1 10.5 %collective-permute-start.5 = (f32[32,2048]{1,0:T(8,128)S(1)}, f32[32,2048]{1,0:T(8,128)}, u32[]{:S(2)}, u32[]{:S(2)}) collective-permute-start(f32[32,2048]{1,0:T(8,128)S(1)} %copy.21), channel_id=1, source_target_pairs={{1,0},{2,1},{3,2},{0,3},{5,4},{6,5},{7,6},{4,7},{9,8},{10,9},{11,1... | collective-permute-start | bytes 786440 | tf_op jit(solution)/shard_map/ppermute | solution.py:26
  126.4 8.9 %collective-permute-start.4 = (f32[32,2048]{1,0:T(8,128)}, f32[32,2048]{1,0:T(8,128)}, u32[]{:S(2)}, u32[]{:S(2)}) collective-permute-start(f32[32,2048]{1,0:T(8,128)} %copy.19), channel_id=1, source_target_pairs={{0,1},{1,2},{2,3},{3,0},{4,5},{5,6},{6,7},{7,4},{8,9},{9,10},{10,1... | collective-permute-start | bytes 786440 | tf_op jit(solution)/shard_map/ppermute | solution.py:24
  347.8 2.9 collective-permute-start.6
  349.1 5.8 collective-permute-start.7
  350.9 4.0 copy-start.10
  350.9 4.0 copy-start.13
  350.9 4.0 copy-start.16
  350.9 4.0 copy-start.19
  350.9 4.0 copy-start.22
  351.0 4.0 copy-start.25
  351.0 4.0 copy-start.28
  351.0 4.0 copy-start.31
  351.0 4.0 copy-start.34
  351.0 4.0 copy-start.37
  363.4 8.2 %collective-permute-start.8 = (f32[32,2048]{1,0:T(8,128)S(1)}, f32[32,2048]{1,0:T(8,128)}, u32[]{:S(2)}, u32[]{:S(2)}) collective-permute-start(f32[32,2048]{1,0:T(8,128)S(1)} %copy.23), channel_id=1, source_target_pairs={{0,1},{1,2},{2,3},{3,0},{4,5},{5,6},{6,7},{7,4},{8,9},{9,10},{10,1... | collective-permute-start | bytes 786440 | tf_op jit(solution)/shard_map/ppermute | solution.py:24
  364.5 8.5 %collective-permute-start.9 = (f32[32,2048]{1,0:T(8,128)}, f32[32,2048]{1,0:T(8,128)}, u32[]{:S(2)}, u32[]{:S(2)}) collective-permute-start(f32[32,2048]{1,0:T(8,128)} %copy.25), channel_id=1, source_target_pairs={{1,0},{2,1},{3,2},{0,3},{5,4},{6,5},{7,6},{4,7},{9,8},{10,9},{11,1... | collective-permute-start | bytes 786440 | tf_op jit(solution)/shard_map/ppermute | solution.py:26
  586.8 2.9 collective-permute-start.10
  588.1 5.8 collective-permute-start.11
  602.3 8.4 %collective-permute-start.12 = (f32[32,2048]{1,0:T(8,128)S(1)}, f32[32,2048]{1,0:T(8,128)}, u32[]{:S(2)}, u32[]{:S(2)}) collective-permute-start(f32[32,2048]{1,0:T(8,128)S(1)} %copy.27), channel_id=1, source_target_pairs={{0,1},{1,2},{2,3},{3,0},{4,5},{5,6},{6,7},{7,4},{8,9},{9,10},{10,1... | collective-permute-start | bytes 786440 | tf_op jit(solution)/shard_map/ppermute | solution.py:24
  603.4 8.7 %collective-permute-start.13 = (f32[32,2048]{1,0:T(8,128)}, f32[32,2048]{1,0:T(8,128)}, u32[]{:S(2)}, u32[]{:S(2)}) collective-permute-start(f32[32,2048]{1,0:T(8,128)} %copy.29), channel_id=1, source_target_pairs={{1,0},{2,1},{3,2},{0,3},{5,4},{6,5},{7,6},{4,7},{9,8},{10,9},{11,1... | collective-permute-start | bytes 786440 | tf_op jit(solution)/shard_map/ppermute | solution.py:26
  (30 other events, 91.4 us)
where the time goes:
time: 807 us; the launch traced here: 799 us
  other arithmetic  448 us (56%)
  blocking collectives  151 us (19%)
  local copies, waits for them, and re-layouts  128 us (16%)
  waiting for transfers between devices  24.5 us (3%)
  starting transfers between devices  23.1 us (3%)
  matrix products  15.5 us (2%)
  between operations  8.42 us (1%)
    reduce_sum x3, other arithmetic, on_device(): alpha = norm_now / lax.psum(jnp.sum(direction * image), ('cells', 'tm'))  420 us
    gather x2, local copies, waits for them, and re-layouts, on_device(): region_pair = jnp.take(region_padded, local_index)  90.5 us
    psum x3, blocking collectives, squares(): return lax.psum(jnp.sum(residual * residual), ('cells', 'tm'))  90.4 us
    psum x2, blocking collectives, on_device(): alpha = norm_now / lax.psum(jnp.sum(direction * image), ('cells', 'tm'))  60.3 us
    ppermute x7, waiting for transfers between devices, extended(): lax.ppermute(tail, axis, [(i, (i + 1) % count) for i in range(ends)])  17 us
  transfers between devices with their start and end apart: 14, of which 6 were waited for; matrix products, arithmetic and copies ran while one was open for 14% of the time, Pallas kernels for 0%

commit v1 on v0

v1 whole, which is shorter than its diff:
```python
import functools

import jax
import jax.numpy as jnp
from jax import lax
from jax.experimental import pallas as pl
from jax.experimental.pallas import tpu as pltpu
from jax.sharding import PartitionSpec as P

MESH = pl.DeviceIdType.MESH
W = 32
HB = 32
ITERS = 3
PAIR = 0.075
DIAG = 2.0
TAP_TOTAL = 0.9
SHIFT = 2.3
TAU = 4.0
L = 128
CH = 256
F32 = jnp.float32
BF16 = jnp.bfloat16


def split(values):
    high = values.astype(BF16)
    return high, (values - high.astype(F32)).astype(BF16)


def dot(a, b):
    return jnp.dot(a, b, preferred_element_type=F32)


def combine(factors, vectors):
    total = factors[0] * vectors[0]
    for factor, vector in zip(factors[1:], vectors[1:]):
        total = total + factor * vector
    return total


def polynomial_steps(moments):
    def form(left, right, up):
        total = None
        for i, a in enumerate(left):
            for j, b in enumerate(right):
                term = a * b * moments[i + j + up]
                total = term if total is None else total + term
        return total

    zero = jnp.zeros_like(moments[0])
    residual = [zero + 1.0]
    direction = [zero + 1.0]
    iterate = [zero] * ITERS
    norm_now = moments[0]
    for count in range(ITERS):
        alpha = norm_now / (SHIFT * form(direction, direction, 0) + TAU * form(direction, direction, 1))
        image = [zero] * (len(direction) + 1)
        for k, value in enumerate(direction):
            image[k] = image[k] + SHIFT * value
            image[k + 1] = image[k + 1] + TAU * value
            iterate[k] = iterate[k] + alpha * value
        residual = residual + [zero] * (len(image) - len(residual))
        residual = [r - alpha * q for r, q in zip(residual, image)]
        if count + 1 < ITERS:
            norm_next = form(residual, residual, 0)
            beta = norm_next / norm_now
            padded = direction + [zero] * (len(residual) - len(direction))
            direction = [r + beta * d for r, d in zip(residual, padded)]
            norm_now = norm_next
    return iterate, residual


def kernel(
    n_cells, n_tm,
    taps, observed, mask, noise, spread, neighbours, regions,
    solution_out, residual_out,
    basis, scaled, counts, toeplitz, edge_t, column_ids, region_row, region_send, region_recv,
    day_send, day_recv, cell_send, cell_recv, partial, moments, gather_tm, gather_cells,
    day_ssem, day_rsem, cell_ssem, cell_rsem, region_ssem, region_rsem,
    tm_ssem, tm_rsem, cells_ssem, cells_rsem,
):
    days, tile = observed.shape
    chunks = tile // CH
    slots = neighbours.shape[0]
    my_cells = lax.axis_index("cells")
    my_tm = lax.axis_index("tm")
    after = lax.rem(my_tm + 1, n_tm)
    before = lax.rem(my_tm + n_tm - 1, n_tm)
    has_left = my_cells > 0
    has_right = my_cells < n_cells - 1

    barrier = pltpu.get_barrier_semaphore()
    for step in range(1, n_tm):
        pl.semaphore_signal(
            barrier, inc=1, device_id={"tm": lax.rem(my_tm + step, n_tm)}, device_id_type=MESH
        )
    for step in range(1, n_cells):
        pl.semaphore_signal(
            barrier, inc=1, device_id={"cells": lax.rem(my_cells + step, n_cells)}, device_id_type=MESH
        )
    pl.semaphore_wait(barrier, n_tm + n_cells - 2)

    def to_cells(source, target, ssem, rsem, peer):
        return pltpu.make_async_remote_copy(
            src_ref=source, dst_ref=target, send_sem=ssem, recv_sem=rsem,
            device_id={"cells": peer}, device_id_type=MESH,
        )

    def to_tm(source, target, ssem, rsem, peer):
        return pltpu.make_async_remote_copy(
            src_ref=source, dst_ref=target, send_sem=ssem, recv_sem=rsem,
            device_id={"tm": peer}, device_id_type=MESH,
        )

    def cell_copies(buffer_s, buffer_r, ssem, rsem):
        leftward = to_cells(
            buffer_s.at[0], buffer_r.at[1], ssem.at[0], rsem.at[1], jnp.maximum(my_cells - 1, 0)
        )
        rightward = to_cells(
            buffer_s.at[1], buffer_r.at[0], ssem.at[1], rsem.at[0], jnp.minimum(my_cells + 1, n_cells - 1)
        )
        return leftward, rightward

    def start_cells(copies):
        @pl.when(has_left)
        def _():
            copies[0].start()

        @pl.when(has_right)
        def _():
            copies[1].start()

    def wait_cells(copies):
        @pl.when(has_left)
        def _():
            copies[0].wait_send()
            copies[1].wait_recv()

        @pl.when(has_right)
        def _():
            copies[1].wait_send()
            copies[0].wait_recv()

    region_send[0] = jnp.broadcast_to(regions[:, :L], (8, L))
    region_send[1] = jnp.broadcast_to(regions[:, tile - L :], (8, L))
    region_copies = cell_copies(region_send, region_recv, region_ssem, region_rsem)
    start_cells(region_copies)

    lanes = lax.broadcasted_iota(jnp.int32, (days // 4, L), 1)

    def columns(chunk):
        return pl.ds(pl.multiple_of(chunk * CH, CH), CH)

    def store_scaled(chunk, vector):
        high, low = split(vector * spread[:, columns(chunk)])
        place = pl.ds(pl.multiple_of(L + chunk * CH, L), CH)
        scaled[:days, place] = high
        scaled[days:, place] = low

    def send_edges(level):
        quarter = days // 4
        left = basis[level, :, :L] * spread[:, :L]
        right = basis[level, :, tile - L :] * spread[:, tile - L :]
        for side, block in ((0, left), (1, right)):
            packed = None
            for q in range(4):
                part = block[q * quarter : (q + 1) * quarter]
                shift = (q * HB - (0 if side == 0 else L - HB)) % L
                part = pltpu.roll(part, shift, 1) if shift else part
                packed = part if packed is None else jnp.where(lanes >= q * HB, part, packed)
            cell_send[level, side] = packed
        copies = cell_copies(
            cell_send.at[level], cell_recv.at[level], cell_ssem.at[level], cell_rsem.at[level]
        )
        start_cells(copies)
        return copies

    def take_edges(level, copies):
        quarter = days // 4
        wait_cells(copies)
        for side, flag, base in ((0, has_left, 0), (1, has_right, L + tile)):

            @pl.when(flag)
            def _(side=side, base=base):
                packed = cell_recv[level, side]
                for q in range(4):
                    shift = ((L - HB if side == 0 else 0) - q * HB) % L
                    part = pltpu.roll(packed, shift, 1) if shift else packed
                    keep = lanes >= L - HB if side == 0 else lanes < HB
                    high, low = split(jnp.where(keep, part, 0.0))
                    scaled[q * quarter : (q + 1) * quarter, base : base + L] = high
                    scaled[days + q * quarter : days + (q + 1) * quarter, base : base + L] = low

    scaled[:, :L] = jnp.zeros((2 * days, L), BF16)
    scaled[:, L + tile :] = jnp.zeros((2 * days, L), BF16)

    @pl.loop(0, chunks)
    def _(chunk):
        value = observed[:, columns(chunk)] * mask[:, columns(chunk)].astype(F32)
        basis[0, :, columns(chunk)] = value
        store_scaled(chunk, value)

    copies = send_edges(0)

    region_row[:, L : L + tile] = regions[...]

    def column_block(block):
        row = region_row[:, pl.ds(pl.multiple_of(block * L, L), L)]
        column_ids[pl.ds(pl.multiple_of(block * L, L), L), :] = jnp.broadcast_to(row, (L, L)).T

    @pl.loop(1, 1 + tile // L)
    def _(block):
        column_block(block)

    span = L + 2 * HB
    span_ids = lax.broadcasted_iota(jnp.int32, (span, L), 0)

    def count_chunk(chunk):
        counts[chunk] = jnp.zeros((2 * CH, CH), BF16)
        for half in range(2):
            start = chunk * CH + half * L
            place = pl.ds(pl.multiple_of(start, L), L)
            ids = span_ids + (my_cells * tile + start - HB)
            found = jnp.zeros((span, L), F32)
            for slot in range(slots):
                found = jnp.where(ids == neighbours[pl.ds(slot, 1), place], found + 1.0, found)
            same = column_ids[pl.ds(pl.multiple_of(start + L - HB, HB), span), :] == regions[:, place]
            found = jnp.where(same, found, 0.0)
            counts[chunk, half * L + L - HB : half * L + L - HB + span, half * L : half * L + L] = found.astype(BF16)

    @pl.loop(1, chunks - 1)
    def _(chunk):
        count_chunk(chunk)

    gap = jnp.abs(
        lax.broadcasted_iota(jnp.int32, (days, days), 0) - lax.broadcasted_iota(jnp.int32, (days, days), 1)
    )
    gap_prev = lax.broadcasted_iota(jnp.int32, (W, W), 0) + W - lax.broadcasted_iota(jnp.int32, (W, W), 1)
    gap_next = lax.broadcasted_iota(jnp.int32, (W, W), 1) + W - lax.broadcasted_iota(jnp.int32, (W, W), 0)

    def tap_values(distance):
        def body(k, value):
            return jnp.where(distance == k + 1, taps[k] * (TAP_TOTAL / W / TAU), value)

        return lax.fori_loop(0, W, body, jnp.zeros(distance.shape, F32))

    for row in range(0, days, 64):
        high, low = split(tap_values(gap[row : row + 64]))
        toeplitz[row : row + 64] = high
        toeplitz[days + row : days + row + 64] = low
    for side, distance in ((0, gap_prev), (1, gap_next)):
        high, low = split(tap_values(distance))
        edge_t[side, :W] = high
        edge_t[side, W:] = low

    wait_cells(region_copies)
    region_row[:, :L] = jnp.where(has_left, region_recv[0, :1], -1)
    region_row[:, L + tile :] = jnp.where(has_right, region_recv[1, :1], -1)
    column_block(0)
    column_block(1 + tile // L)
    count_chunk(0)
    count_chunk(chunks - 1)

    moments[...] = jnp.zeros_like(moments)

    def fold(product):
        total = jnp.sum(product.reshape(days // 8, 8, CH), axis=0)
        return total[:, :L] + total[:, L:]

    def day_copies(level, chunk):
        place = columns(chunk)
        return (
            to_tm(
                day_send.at[level, 0, :, place], day_recv.at[level, 1, :, place],
                day_ssem.at[level, 0, chunk], day_rsem.at[level, 1, chunk], before,
            ),
            to_tm(
                day_send.at[level, 1, :, place], day_recv.at[level, 0, :, place],
                day_ssem.at[level, 1, chunk], day_rsem.at[level, 0, chunk], after,
            ),
        )

    def spatial(level, chunk):
        place = columns(chunk)
        window = scaled[:, pl.ds(pl.multiple_of(chunk * CH, CH), 2 * CH)]
        gathered = dot(window, counts[chunk])
        vector = basis[level, :, place]
        mixed = vector + (PAIR * spread[:, place]) * (gathered[:days] + gathered[days:])
        day_send[level, 0, :, place] = mixed[:W]
        day_send[level, 1, :, place] = mixed[days - W :]
        for copy in day_copies(level, chunk):
            copy.start()
        high, low = split(mixed)
        both = dot(toeplitz[...], high)
        smooth = (DIAG / TAU) * mixed + both[:days] + both[days:] + dot(toeplitz[:days], low)
        basis[level + 1, :, place] = smooth

    def finish(level, chunk):
        place = columns(chunk)
        for copy in day_copies(level, chunk):
            copy.wait()
        for side, rows in ((0, slice(0, W)), (1, slice(days - W, days))):
            high, low = split(day_recv[level, side, :, place])
            both = dot(edge_t[side], high)
            basis[level + 1, rows, place] = (
                basis[level + 1, rows, place] + both[:W] + both[W:] + dot(edge_t[side, :W], low)
            )
        vector = basis[level, :, place]
        image = ((noise[:, place] - SHIFT) * (1.0 / TAU)) * vector + mask[:, place].astype(F32) * basis[
            level + 1, :, place
        ]
        basis[level + 1, :, place] = image
        moments[2 * level] += fold(vector * vector)
        moments[2 * level + 1] += fold(vector * image)
        if level + 1 < ITERS:
            store_scaled(chunk, image)

    for level in range(ITERS):

        @pl.loop(1, chunks - 1)
        def _(chunk):
            spatial(level, chunk)

        take_edges(level, copies)

        @pl.loop(0, 2)
        def _(index):
            spatial(level, index * (chunks - 1))

        @pl.loop(1, chunks - 1)
        def _(chunk):
            finish(level, chunk)

        @pl.loop(0, 2)
        def _(index):
            finish(level, index * (chunks - 1))

        if level + 1 < ITERS:
            copies = send_edges(level + 1)

    row_ids = lax.broadcasted_iota(jnp.int32, (8, L), 0)
    packed = jnp.zeros((8, L), F32)
    for k in range(2 * ITERS):
        packed = jnp.where(row_ids == k, jnp.sum(moments[k], axis=0, keepdims=True), packed)
    partial[0] = packed

    def all_sum(source, gathered, ssem, rsem, me, count, send):
        gathered[me] = source[...]
        for step in range(1, count):
            peer = lax.rem(me + step, count)
            send(source, gathered.at[me], ssem.at[step], rsem.at[me], peer).start()
        for step in range(1, count):
            peer = lax.rem(me + step, count)
            send(source, gathered.at[peer], ssem.at[step], rsem.at[peer], peer).wait()
        total = gathered[0]
        for index in range(1, count):
            total = total + gathered[index]
        return total

    partial[1] = all_sum(partial.at[0], gather_tm, tm_ssem, tm_rsem, my_tm, n_tm, to_tm)
    total = all_sum(partial.at[1], gather_cells, cells_ssem, cells_rsem, my_cells, n_cells, to_cells)
    sums = [
        jnp.broadcast_to(jnp.sum(total[k : k + 1], axis=1, keepdims=True), (1, CH)) for k in range(2 * ITERS)
    ]
    iterate, residual = polynomial_steps(sums)

    @pl.loop(0, chunks)
    def _(chunk):
        place = columns(chunk)
        levels = [basis[k, :, place] for k in range(ITERS + 1)]
        solution_out[:, place] = combine(iterate, levels)
        residual_out[:, place] = combine(residual, levels)


def on_device(n_cells, n_tm, observed, mask, noise, spread, taps, neighbours, regions):
    days, tile = observed.shape
    chunks = tile // CH
    dma = pltpu.SemaphoreType.DMA
    vmem = pl.BlockSpec(memory_space=pltpu.VMEM)
    shape = jax.ShapeDtypeStruct(observed.shape, F32)
    return pl.pallas_call(
        functools.partial(kernel, n_cells, n_tm),
        out_shape=(shape, shape),
        in_specs=[pl.BlockSpec(memory_space=pltpu.SMEM)] + [vmem] * 6,
        out_specs=(vmem, vmem),
        scratch_shapes=[
            pltpu.VMEM((ITERS + 1, days, tile), F32),
            pltpu.VMEM((2 * days, tile + 2 * L), BF16),
            pltpu.VMEM((chunks, 2 * CH, CH), BF16),
            pltpu.VMEM((2 * days, days), BF16),
            pltpu.VMEM((2, 2 * W, W), BF16),
            pltpu.VMEM((tile + 2 * L, L), jnp.int32),
            pltpu.VMEM((1, tile + 2 * L), jnp.int32),
            pltpu.VMEM((2, 8, L), jnp.int32),
            pltpu.VMEM((2, 8, L), jnp.int32),
            pltpu.VMEM((ITERS, 2, W, tile), F32),
            pltpu.VMEM((ITERS, 2, W, tile), F32),
            pltpu.VMEM((ITERS, 2, days // 4, L), F32),
            pltpu.VMEM((ITERS, 2, days // 4, L), F32),
            pltpu.VMEM((2, 8, L), F32),
            pltpu.VMEM((2 * ITERS, 8, L), F32),
            pltpu.VMEM((n_tm, 8, L), F32),
            pltpu.VMEM((n_cells, 8, L), F32),
            dma((ITERS, 2, chunks)),
            dma((ITERS, 2, chunks)),
            dma((ITERS, 2)),
            dma((ITERS, 2)),
            dma((2,)),
            dma((2,)),
            dma((n_tm,)),
            dma((n_tm,)),
            dma((n_cells,)),
            dma((n_cells,)),
        ],
        compiler_params=pltpu.CompilerParams(
            collective_id=0, has_side_effects=True, vmem_limit_bytes=56 * 1024 * 1024
        ),
    )(taps, observed, mask, noise[None, :], spread[None, :], neighbours, regions[None, :])


def solution(mesh):
    return jax.shard_map(
        functools.partial(on_device, mesh.shape["cells"], mesh.shape["tm"]),
        mesh=mesh,
        in_specs=(
            P("tm", ("groups", "cells")),
            P("tm", ("groups", "cells")),
            P(("groups", "cells")),
            P(("groups", "cells")),
            P(),
            P(None, ("groups", "cells")),
            P(("groups", "cells")),
        ),
        out_specs=(P("tm", ("groups", "cells")), P("tm", ("groups", "cells"))),
        check_vma=False,
    )
```

time: 807 us -> 53.8 us (0.07)
  other arithmetic: 448 us -> 0 us
  blocking collectives: 151 us -> 0 us
  local copies, waits for them, and re-layouts: 128 us -> 4.61 us
  Pallas kernels: 0 us -> 48.4 us
  waiting for transfers between devices: 24.5 us -> 0 us
  starting transfers between devices: 23.1 us -> 0 us
  matrix products: 15.5 us -> 0 us
    reduce_sum x5 -> x0, other arithmetic: 429 us -> none  [the longest x3 420 us: on_device(): alpha = norm_now / lax.psum(jnp.sum(direction * image), ('cells', 'tm'))]
    psum x5 -> x0, blocking collectives: 151 us -> none  [the longest x3 90.4 us: squares(): return lax.psum(jnp.sum(residual * residual), ('cells', 'tm'))]
    gather x2 -> x0, local copies, waits for them, and re-layouts: 90.5 us -> none  [on_device(): region_pair = jnp.take(region_padded, local_index)]
    pallas_call x0 -> x1, Pallas kernels: none -> 48.4 us  [on_device(): pl.pallas_call(functools.partial(kernel, n_cells, n_tm), out_shape=(shape...]
    ppermute x14 -> x0, waiting for transfers between devices: 24.5 us -> none  [the longest x7 17 us: extended(): lax.ppermute(tail, axis, [(i, (i + 1) % count) for i in range(ends)])]
    ppermute x14 -> x0, starting transfers between devices: 23.1 us -> none  [the longest x7 13.2 us: extended(): lax.ppermute(tail, axis, [(i, (i + 1) % count) for i in range(ends)])]
    dot_general x3 -> x0, matrix products: 15.5 us -> none  [on_device(): jnp.einsum('tbj,bji->tbi', windows, band, precision=lax.Precision.HIGHEST)]
    slice x17 -> x0, local copies, waits for them, and re-layouts: 14.8 us -> none  [the longest x6 10.2 us: extended(): lax.slice_in_dim(cells, cells.shape[dim] - width, cells.shape[dim], axis=...]
  transfers between devices with their start and end apart: 14 -> 0, of which waited for: 6 -> 0; matrix products, arithmetic and copies ran while one was open for 14% -> 0% of each run, Pallas kernels for 0% -> 0%
where the time goes in v1:
time: 53.8 us; the launch traced here: 53.7 us
  Pallas kernels  48.4 us (90%)
  local copies, waits for them, and re-layouts  4.61 us (9%)
  between operations  0.65 us (1%)
    pallas_call x1, Pallas kernels, on_device(): pl.pallas_call(functools.partial(kernel, n_cells, n_tm), out_shape=(shape...  48.4 us
    unnamed x4, local copies, waits for them, and re-layouts  4.61 us

profile of v1, /device:TPU:0, one launch (start us, length us, event | category | flops | bytes accessed | tf_op | source)
XLA Modules:
  0.0 53.7 jit_solution(7237561947106550883)
XLA Ops:
  0.6 48.4 %shard_map.86 = (f32[256,2048]{1,0:T(8,128)}, f32[256,2048]{1,0:T(8,128)}) custom-call(f32[32]{0:T(128)} %taps.1, f32[256,2048]{1,0:T(8,128)} %observed.1, s32[256,2048]{1,0:T(8,128)} %mask.1, f32[1,2048]{1,0:T(1,128)} %bitcast.3, f32[1,2048]{1,0:T(1,128)} %bitcast.4, s32[8,2048]{1,0:T(8,128)} %neighbours.1, s32[1,2048]{1,0:T(1,128)} %bitcast.5), custom_call_target="tpu_custom_call" | custom-call | tf_op jit(solution)/shard_map/pallas_call | solution.py:381
  49.1 0.0 copy-start
  49.1 3.3 %copy.11 = f32[256,2048]{1,0:T(8,128)} copy(f32[256,2048]{1,0:T(8,128)} %get-tuple-element.4) | data formatting | bytes 4194304
  52.3 0.0 copy-done
  52.3 1.3 %copy.12 = f32[256,2048]{1,0:T(8,128)} copy(f32[256,2048]{1,0:T(8,128)S(1)} %copy-done) | data formatting | bytes 4194304
Async XLA Ops:
  49.1 3.3 %copy-start = (f32[256,2048]{1,0:T(8,128)S(1)}, f32[256,2048]{1,0:T(8,128)}, u32[]{:S(2)}) copy-start(f32[256,2048]{1,0:T(8,128)} %get-tuple-element.5) | copy-start | bytes 6291460

commit v2 on v1

--- a/solution.py
+++ b/solution.py
@@ -38,7 +38,7 @@
     return total
 
 
-def polynomial_steps(moments):
+def polynomial_steps(moments, rho):
     def form(left, right, up):
         total = None
         for i, a in enumerate(left):
@@ -53,10 +53,10 @@
     iterate = [zero] * ITERS
     norm_now = moments[0]
     for count in range(ITERS):
-        alpha = norm_now / (SHIFT * form(direction, direction, 0) + TAU * form(direction, direction, 1))
+        alpha = norm_now / (rho * form(direction, direction, 0) + TAU * form(direction, direction, 1))
         image = [zero] * (len(direction) + 1)
         for k, value in enumerate(direction):
-            image[k] = image[k] + SHIFT * value
+            image[k] = image[k] + rho * value
             image[k + 1] = image[k + 1] + TAU * value
             iterate[k] = iterate[k] + alpha * value
         residual = residual + [zero] * (len(image) - len(residual))
@@ -72,12 +72,12 @@
 
 def kernel(
     n_cells, n_tm,
-    taps, observed, mask, noise, spread, neighbours, regions,
-    solution_out, residual_out,
-    basis, scaled, counts, toeplitz, edge_t, column_ids, region_row, region_send, region_recv,
-    day_send, day_recv, cell_send, cell_recv, partial, moments, gather_tm, gather_cells,
+    taps, observed_hbm, mask_hbm, noise, spread, neighbours, regions,
+    basis_out, factors_out,
+    observed, mask, basis, scaled, counts, toeplitz, edge_t, column_ids, region_row, region_send, region_recv,
+    day_send, day_recv, cell_send, cell_recv, partial, moments, gather_tm, gather_cells, lead,
     day_ssem, day_rsem, cell_ssem, cell_rsem, region_ssem, region_rsem,
-    tm_ssem, tm_rsem, cells_ssem, cells_rsem,
+    tm_ssem, tm_rsem, cells_ssem, cells_rsem, load_sem, store_sem,
 ):
     days, tile = observed.shape
     chunks = tile // CH
@@ -98,7 +98,12 @@
         pl.semaphore_signal(
             barrier, inc=1, device_id={"cells": lax.rem(my_cells + step, n_cells)}, device_id_type=MESH
         )
-    pl.semaphore_wait(barrier, n_tm + n_cells - 2)
+    loads = (
+        pltpu.make_async_copy(observed_hbm, observed, load_sem.at[0]),
+        pltpu.make_async_copy(mask_hbm, mask, load_sem.at[1]),
+    )
+    for load in loads:
+        load.start()
 
     def to_cells(source, target, ssem, rsem, peer):
         return pltpu.make_async_remote_copy(
@@ -140,11 +145,6 @@
         def _():
             copies[1].wait_send()
             copies[0].wait_recv()
-
-    region_send[0] = jnp.broadcast_to(regions[:, :L], (8, L))
-    region_send[1] = jnp.broadcast_to(regions[:, tile - L :], (8, L))
-    region_copies = cell_copies(region_send, region_recv, region_ssem, region_rsem)
-    start_cells(region_copies)
 
     lanes = lax.broadcasted_iota(jnp.int32, (days // 4, L), 1)
 
@@ -191,26 +191,11 @@
                     scaled[q * quarter : (q + 1) * quarter, base : base + L] = high
                     scaled[days + q * quarter : days + (q + 1) * quarter, base : base + L] = low
 
-    scaled[:, :L] = jnp.zeros((2 * days, L), BF16)
-    scaled[:, L + tile :] = jnp.zeros((2 * days, L), BF16)
-
-    @pl.loop(0, chunks)
-    def _(chunk):
-        value = observed[:, columns(chunk)] * mask[:, columns(chunk)].astype(F32)
-        basis[0, :, columns(chunk)] = value
-        store_scaled(chunk, value)
-
-    copies = send_edges(0)
-
     region_row[:, L : L + tile] = regions[...]
 
     def column_block(block):
         row = region_row[:, pl.ds(pl.multiple_of(block * L, L), L)]
         column_ids[pl.ds(pl.multiple_of(block * L, L), L), :] = jnp.broadcast_to(row, (L, L)).T
-
-    @pl.loop(1, 1 + tile // L)
-    def _(block):
-        column_block(block)
 
     span = L + 2 * HB
     span_ids = lax.broadcasted_iota(jnp.int32, (span, L), 0)
@@ -228,10 +213,6 @@
             found = jnp.where(same, found, 0.0)
             counts[chunk, half * L + L - HB : half * L + L - HB + span, half * L : half * L + L] = found.astype(BF16)
 
-    @pl.loop(1, chunks - 1)
-    def _(chunk):
-        count_chunk(chunk)
-
     gap = jnp.abs(
         lax.broadcasted_iota(jnp.int32, (days, days), 0) - lax.broadcasted_iota(jnp.int32, (days, days), 1)
     )
@@ -253,13 +234,30 @@
         edge_t[side, :W] = high
         edge_t[side, W:] = low
 
-    wait_cells(region_copies)
-    region_row[:, :L] = jnp.where(has_left, region_recv[0, :1], -1)
-    region_row[:, L + tile :] = jnp.where(has_right, region_recv[1, :1], -1)
-    column_block(0)
-    column_block(1 + tile // L)
-    count_chunk(0)
-    count_chunk(chunks - 1)
+    @pl.loop(1, 1 + tile // L)
+    def _(block):
+        column_block(block)
+
+    pl.semaphore_wait(barrier, n_tm + n_cells - 2)
+
+    region_send[0] = jnp.broadcast_to(regions[:, :L], (8, L))
+    region_send[1] = jnp.broadcast_to(regions[:, tile - L :], (8, L))
+    region_copies = cell_copies(region_send, region_recv, region_ssem, region_rsem)
+    start_cells(region_copies)
+
+    scaled[:, :L] = jnp.zeros((2 * days, L), BF16)
+    scaled[:, L + tile :] = jnp.zeros((2 * days, L), BF16)
+
+    for load in loads:
+        load.wait()
+
+    @pl.loop(0, chunks)
+    def _(chunk):
+        value = observed[:, columns(chunk)] * mask[:, columns(chunk)].astype(F32)
+        basis[0, :, columns(chunk)] = value
+        store_scaled(chunk, value)
+
+    copies = send_edges(0)
 
     moments[...] = jnp.zeros_like(moments)
 
@@ -309,46 +307,29 @@
         image = ((noise[:, place] - SHIFT) * (1.0 / TAU)) * vector + mask[:, place].astype(F32) * basis[
             level + 1, :, place
         ]
+        if level == 1:
+            start = basis[0, :, place]
+            other = vector - lead[:, :CH] * start
+            image = image - lead[:, :CH] * (vector + other)
+            vector = other
+            basis[1, :, place] = vector
+        elif level == 2:
+            image = image - lead[:, :CH] * vector
         basis[level + 1, :, place] = image
         moments[2 * level] += fold(vector * vector)
         moments[2 * level + 1] += fold(vector * image)
         if level + 1 < ITERS:
             store_scaled(chunk, image)
 
-    for level in range(ITERS):
-
-        @pl.loop(1, chunks - 1)
-        def _(chunk):
-            spatial(level, chunk)
-
-        take_edges(level, copies)
-
-        @pl.loop(0, 2)
-        def _(index):
-            spatial(level, index * (chunks - 1))
-
-        @pl.loop(1, chunks - 1)
-        def _(chunk):
-            finish(level, chunk)
-
-        @pl.loop(0, 2)
-        def _(index):
-            finish(level, index * (chunks - 1))
-
-        if level + 1 < ITERS:
-            copies = send_edges(level + 1)
-
     row_ids = lax.broadcasted_iota(jnp.int32, (8, L), 0)
-    packed = jnp.zeros((8, L), F32)
-    for k in range(2 * ITERS):
-        packed = jnp.where(row_ids == k, jnp.sum(moments[k], axis=0, keepdims=True), packed)
-    partial[0] = packed
-
-    def all_sum(source, gathered, ssem, rsem, me, count, send):
+
+    def start_sum(source, gathered, ssem, rsem, me, count, send):
         gathered[me] = source[...]
         for step in range(1, count):
             peer = lax.rem(me + step, count)
             send(source, gathered.at[me], ssem.at[step], rsem.at[me], peer).start()
+
+    def end_sum(source, gathered, ssem, rsem, me, count, send):
         for step in range(1, count):
             peer = lax.rem(me + step, count)
             send(source, gathered.at[peer], ssem.at[step], rsem.at[peer], peer).wait()
@@ -357,19 +338,107 @@
             total = total + gathered[index]
         return total
 
-    partial[1] = all_sum(partial.at[0], gather_tm, tm_ssem, tm_rsem, my_tm, n_tm, to_tm)
-    total = all_sum(partial.at[1], gather_cells, cells_ssem, cells_rsem, my_cells, n_cells, to_cells)
-    sums = [
-        jnp.broadcast_to(jnp.sum(total[k : k + 1], axis=1, keepdims=True), (1, CH)) for k in range(2 * ITERS)
-    ]
-    iterate, residual = polynomial_steps(sums)
-
-    @pl.loop(0, chunks)
-    def _(chunk):
-        place = columns(chunk)
-        levels = [basis[k, :, place] for k in range(ITERS + 1)]
-        solution_out[:, place] = combine(iterate, levels)
-        residual_out[:, place] = combine(residual, levels)
+    def over_tm(turn):
+        return (partial.at[turn, 0], gather_tm.at[turn], tm_ssem.at[turn], tm_rsem.at[turn], my_tm, n_tm, to_tm)
+
+    def over_cells(turn):
+        return (
+            partial.at[turn, 1], gather_cells.at[turn], cells_ssem.at[turn], cells_rsem.at[turn],
+            my_cells, n_cells, to_cells,
+        )
+
+    def sums_begin(turn, first, last):
+        packed = jnp.zeros((8, L), F32)
+        for k in range(first, last):
+            packed = jnp.where(row_ids == k, jnp.sum(moments[k], axis=0, keepdims=True), packed)
+        partial[turn, 0] = packed
+        start_sum(*over_tm(turn))
+
+    def sums_middle(turn):
+        partial[turn, 1] = end_sum(*over_tm(turn))
+        start_sum(*over_cells(turn))
+
+    def sums_end(turn, first, last):
+        total = end_sum(*over_cells(turn))
+        return [
+            jnp.broadcast_to(jnp.sum(total[k : k + 1], axis=1, keepdims=True), (1, CH))
+            for k in range(first, last)
+        ]
+
+    def save(level):
+        return pltpu.make_async_copy(basis.at[level], basis_out.at[level], store_sem.at[level])
+
+    last = chunks - 1
+    outer = (1, last - 1, 0, last)
+    inner = [c for k in range(2, chunks // 2) for c in (k, last - k)]
+
+    for chunk in outer[:2]:
+        count_chunk(chunk)
+        spatial(0, chunk)
+    wait_cells(region_copies)
+    region_row[:, :L] = jnp.where(has_left, region_recv[0, :1], -1)
+    region_row[:, L + tile :] = jnp.where(has_right, region_recv[1, :1], -1)
+    column_block(0)
+    column_block(1 + tile // L)
+    take_edges(0, copies)
+    for chunk in outer[2:]:
+        count_chunk(chunk)
+        spatial(0, chunk)
+    for chunk in inner:
+        count_chunk(chunk)
+        spatial(0, chunk)
+
+    factor_now = None
+    for level in range(ITERS - 1):
+        if level == 1:
+            sums = sums_end(0, 0, 2)
+            factor_now = sums[1] / sums[0]
+            lead[...] = factor_now
+            norm_first = sums[0]
+        for chunk in outer:
+            finish(level, chunk)
+        copies = send_edges(level + 1)
+        for low, high in ((2, 1), (last - 2, last - 1)):
+            finish(level, low)
+            spatial(level + 1, high)
+        take_edges(level + 1, copies)
+        spatial(level + 1, 0)
+        spatial(level + 1, last)
+        rest = inner[2:]
+        for chunk in rest:
+            finish(level, chunk)
+        save(level).start()
+        if level == 0:
+            sums_begin(0, 0, 2)
+        half = len(inner) // 2
+        for chunk in inner[:half]:
+            spatial(level + 1, chunk)
+        if level == 0:
+            sums_middle(0)
+        for chunk in inner[half:]:
+            spatial(level + 1, chunk)
+    save(ITERS - 1).start()
+    for chunk in outer:
+        finish(ITERS - 1, chunk)
+    for chunk in inner:
+        finish(ITERS - 1, chunk)
+    save(ITERS).start()
+    sums_begin(1, 2, 2 * ITERS)
+    sums_middle(1)
+    rho = SHIFT + TAU * factor_now
+    tail = sums_end(1, 2, 2 * ITERS)
+    iterate, residual = polynomial_steps([norm_first, jnp.zeros_like(norm_first)] + tail, rho)
+    for k, value in enumerate(iterate + residual):
+        factors_out[pl.ds(k, 1), :] = value[:, :L]
+    factors_out[pl.ds(2 * ITERS + 1, 1), :] = jnp.zeros((1, L), F32)
+    for level in range(ITERS + 1):
+        save(level).wait()
+
+
+def combine_kernel(factors, basis, solution_out, residual_out):
+    levels = [basis[k] for k in range(ITERS + 1)]
+    solution_out[...] = combine([factors[k, 0] for k in range(ITERS)], levels)
+    residual_out[...] = combine([factors[k, 0] for k in range(ITERS, 2 * ITERS + 1)], levels)
 
 
 def on_device(n_cells, n_tm, observed, mask, noise, spread, taps, neighbours, regions):
@@ -378,12 +447,17 @@
     dma = pltpu.SemaphoreType.DMA
     vmem = pl.BlockSpec(memory_space=pltpu.VMEM)
     shape = jax.ShapeDtypeStruct(observed.shape, F32)
-    return pl.pallas_call(
+    basis, factors = pl.pallas_call(
         functools.partial(kernel, n_cells, n_tm),
-        out_shape=(shape, shape),
-        in_specs=[pl.BlockSpec(memory_space=pltpu.SMEM)] + [vmem] * 6,
-        out_specs=(vmem, vmem),
+        out_shape=(
+            jax.ShapeDtypeStruct((ITERS + 1, days, tile), F32),
+            jax.ShapeDtypeStruct((8, L), F32),
+        ),
+        in_specs=[pl.BlockSpec(memory_space=pltpu.SMEM)] + [pl.BlockSpec(memory_space=pl.ANY)] * 2 + [vmem] * 4,
+        out_specs=(pl.BlockSpec(memory_space=pl.ANY), vmem),
         scratch_shapes=[
+            pltpu.VMEM((days, tile), F32),
+            pltpu.VMEM((days, tile), jnp.int32),
             pltpu.VMEM((ITERS + 1, days, tile), F32),
             pltpu.VMEM((2 * days, tile + 2 * L), BF16),
             pltpu.VMEM((chunks, 2 * CH, CH), BF16),
@@ -397,25 +471,40 @@
             pltpu.VMEM((ITERS, 2, W, tile), F32),
             pltpu.VMEM((ITERS, 2, days // 4, L), F32),
             pltpu.VMEM((ITERS, 2, days // 4, L), F32),
-            pltpu.VMEM((2, 8, L), F32),
+            pltpu.VMEM((2, 2, 8, L), F32),
             pltpu.VMEM((2 * ITERS, 8, L), F32),
-            pltpu.VMEM((n_tm, 8, L), F32),
-            pltpu.VMEM((n_cells, 8, L), F32),
+            pltpu.VMEM((2, n_tm, 8, L), F32),
+            pltpu.VMEM((2, n_cells, 8, L), F32),
+            pltpu.VMEM((1, CH), F32),
             dma((ITERS, 2, chunks)),
             dma((ITERS, 2, chunks)),
             dma((ITERS, 2)),
             dma((ITERS, 2)),
             dma((2,)),
             dma((2,)),
-            dma((n_tm,)),
-            dma((n_tm,)),
-            dma((n_cells,)),
-            dma((n_cells,)),
+            dma((2, n_tm)),
+            dma((2, n_tm)),
+            dma((2, n_cells)),
+            dma((2, n_cells)),
+            dma((2,)),
+            dma((ITERS + 1,)),
         ],
         compiler_params=pltpu.CompilerParams(
             collective_id=0, has_side_effects=True, vmem_limit_bytes=56 * 1024 * 1024
         ),
     )(taps, observed, mask, noise[None, :], spread[None, :], neighbours, regions[None, :])
+    rows = 32
+    block = pl.BlockSpec((rows, tile), lambda i: (i, 0))
+    return pl.pallas_call(
+        combine_kernel,
+        grid=(days // rows,),
+        out_shape=(shape, shape),
+        in_specs=[
+            pl.BlockSpec(memory_space=pltpu.SMEM),
+            pl.BlockSpec((ITERS + 1, rows, tile), lambda i: (0, i, 0)),
+        ],
+        out_specs=(block, block),
+    )(factors, basis)
 
 
 def solution(mesh):

time: 53.8 us -> 54.5 us (1.013)
  Pallas kernels: 48.4 us -> 53.5 us
  local copies, waits for them, and re-layouts: 4.61 us -> 0 us
    pallas_call x1 -> x2, Pallas kernels: 48.4 us -> 53.5 us  [the longest x1 45.8 us: on_device(): pl.pallas_call(functools.partial(kernel, n_cells, n_tm), out_shape=(jax.S...]
    unnamed x4 -> x0, local copies, waits for them, and re-layouts: 4.61 us -> none
where the time goes in v2:
time: 54.5 us; the launch traced here: 54.1 us
  Pallas kernels  53.5 us (98%)
  between operations  0.64 us (1%)
    pallas_call x1, Pallas kernels, on_device(): pl.pallas_call(functools.partial(kernel, n_cells, n_tm), out_shape=(jax.S...  45.8 us
    pallas_call x1, Pallas kernels, on_device(): pl.pallas_call(combine_kernel, grid=(days // rows,), out_shape=(shape, sh...  7.7 us

profile of v2, /device:TPU:0, one launch (start us, length us, event | category | flops | bytes accessed | tf_op | source)
XLA Modules:
  0.0 54.1 jit_solution(6507069636674405981)
XLA Ops:
  0.6 45.8 %shard_map.86 = (f32[4,256,2048]{2,1,0:T(8,128)}, f32[8,128]{1,0:T(8,128)}) custom-call(f32[32]{0:T(128)} %taps.1, f32[256,2048]{1,0:T(8,128)} %observed_hbm.1, s32[256,2048]{1,0:T(8,128)} %mask_hbm.1, f32[1,2048]{1,0:T(1,128)} %bitcast.3, f32[1,2048]{1,0:T(1,128)} %bitcast.4, s32[8,2048]{1,0:T(8,128)} %neighbours.1, s32[1,2048]{1,0:T(1,128)} %bitcast.5), custom_call_target="tpu_custom_call" | custom-call | tf_op jit(solution)/shard_map/pallas_call | solution.py:450
  46.4 7.7 %shard_map.87 = (f32[256,2048]{1,0:T(8,128)}, f32[256,2048]{1,0:T(8,128)}) custom-call(f32[8,128]{1,0:T(8,128)} %get-tuple-element.4.factors, f32[4,256,2048]{2,1,0:T(8,128)} %get-tuple-element.5.basis), custom_call_target="tpu_custom_call" | custom-call | tf_op jit(solution)/shard_map/pallas_call | solution.py:498

commit v3 on v2

--- a/solution.py
+++ b/solution.py
@@ -149,11 +149,12 @@
     lanes = lax.broadcasted_iota(jnp.int32, (days // 4, L), 1)
 
     def columns(chunk):
-        return pl.ds(pl.multiple_of(chunk * CH, CH), CH)
+        return pl.ds(chunk * CH if isinstance(chunk, int) else pl.multiple_of(chunk * CH, CH), CH)
 
     def store_scaled(chunk, vector):
         high, low = split(vector * spread[:, columns(chunk)])
-        place = pl.ds(pl.multiple_of(L + chunk * CH, L), CH)
+        start = L + chunk * CH
+        place = pl.ds(start if isinstance(chunk, int) else pl.multiple_of(start, L), CH)
         scaled[:days, place] = high
         scaled[days:, place] = low
 
@@ -193,9 +194,13 @@
 
     region_row[:, L : L + tile] = regions[...]
 
+    eye = lax.broadcasted_iota(jnp.int32, (L, L), 0) == lax.broadcasted_iota(jnp.int32, (L, L), 1)
+    ones = jnp.ones((L, L), BF16)
+
     def column_block(block):
-        row = region_row[:, pl.ds(pl.multiple_of(block * L, L), L)]
-        column_ids[pl.ds(pl.multiple_of(block * L, L), L), :] = jnp.broadcast_to(row, (L, L)).T
+        row = region_row[:, block * L : (block + 1) * L].astype(F32)
+        diagonal = jnp.where(eye, row, 0.0).astype(BF16)
+        column_ids[block * L : (block + 1) * L, :] = dot(diagonal, ones)
 
     span = L + 2 * HB
     span_ids = lax.broadcasted_iota(jnp.int32, (span, L), 0)
@@ -204,38 +209,35 @@
         counts[chunk] = jnp.zeros((2 * CH, CH), BF16)
         for half in range(2):
             start = chunk * CH + half * L
-            place = pl.ds(pl.multiple_of(start, L), L)
+            place = pl.ds(start, L)
             ids = span_ids + (my_cells * tile + start - HB)
             found = jnp.zeros((span, L), F32)
             for slot in range(slots):
                 found = jnp.where(ids == neighbours[pl.ds(slot, 1), place], found + 1.0, found)
-            same = column_ids[pl.ds(pl.multiple_of(start + L - HB, HB), span), :] == regions[:, place]
+            same = column_ids[start + L - HB : start + L - HB + span, :] == regions[:, place].astype(F32)
             found = jnp.where(same, found, 0.0)
             counts[chunk, half * L + L - HB : half * L + L - HB + span, half * L : half * L + L] = found.astype(BF16)
 
+    rows_t = 2 * W
     gap = jnp.abs(
-        lax.broadcasted_iota(jnp.int32, (days, days), 0) - lax.broadcasted_iota(jnp.int32, (days, days), 1)
+        lax.broadcasted_iota(jnp.int32, (rows_t, L), 0) + W - lax.broadcasted_iota(jnp.int32, (rows_t, L), 1)
     )
-    gap_prev = lax.broadcasted_iota(jnp.int32, (W, W), 0) + W - lax.broadcasted_iota(jnp.int32, (W, W), 1)
-    gap_next = lax.broadcasted_iota(jnp.int32, (W, W), 1) + W - lax.broadcasted_iota(jnp.int32, (W, W), 0)
-
-    def tap_values(distance):
-        def body(k, value):
-            return jnp.where(distance == k + 1, taps[k] * (TAP_TOTAL / W / TAU), value)
-
-        return lax.fori_loop(0, W, body, jnp.zeros(distance.shape, F32))
-
-    for row in range(0, days, 64):
-        high, low = split(tap_values(gap[row : row + 64]))
-        toeplitz[row : row + 64] = high
-        toeplitz[days + row : days + row + 64] = low
-    for side, distance in ((0, gap_prev), (1, gap_next)):
-        high, low = split(tap_values(distance))
-        edge_t[side, :W] = high
-        edge_t[side, W:] = low
-
-    @pl.loop(1, 1 + tile // L)
-    def _(block):
+    band = jnp.zeros((rows_t, L), F32)
+    for k in range(W):
+        band = jnp.where(gap == k + 1, taps[k] * (TAP_TOTAL / W / TAU), band)
+    wide = jnp.concatenate([band, jnp.zeros((rows_t, days - L), F32)], axis=1)
+    lanes_t = lax.broadcasted_iota(jnp.int32, (rows_t, days), 1)
+    for row in range(0, days, rows_t):
+        shift = (row - W) % days
+        near = pltpu.roll(wide, shift, 1) if shift else wide
+        near = jnp.where((lanes_t >= row - W) & (lanes_t < row + rows_t + W), near, 0.0)
+        high, low = split(near)
+        toeplitz[row : row + rows_t] = jnp.concatenate([high, low, high], axis=1)
+    for side, part in ((0, band[:W, :W]), (1, band[W:, L - W :])):
+        high, low = split(part)
+        edge_t[side] = jnp.concatenate([high, low, high], axis=1)
+
+    for block in range(1, 1 + tile // L):
         column_block(block)
 
     pl.semaphore_wait(barrier, n_tm + n_cells - 2)
@@ -265,48 +267,68 @@
         total = jnp.sum(product.reshape(days // 8, 8, CH), axis=0)
         return total[:, :L] + total[:, L:]
 
-    def day_copies(level, chunk):
-        place = columns(chunk)
+    def day_copies(level, group):
+        place = pl.ds(group * 2 * CH, 2 * CH)
         return (
             to_tm(
                 day_send.at[level, 0, :, place], day_recv.at[level, 1, :, place],
-                day_ssem.at[level, 0, chunk], day_rsem.at[level, 1, chunk], before,
+                day_ssem.at[level, 0, group], day_rsem.at[level, 1, group], before,
             ),
             to_tm(
                 day_send.at[level, 1, :, place], day_recv.at[level, 0, :, place],
-                day_ssem.at[level, 1, chunk], day_rsem.at[level, 0, chunk], after,
+                day_ssem.at[level, 1, group], day_rsem.at[level, 0, group], after,
             ),
         )
 
-    def spatial(level, chunk):
+    def gather(level, chunk):
         place = columns(chunk)
-        window = scaled[:, pl.ds(pl.multiple_of(chunk * CH, CH), 2 * CH)]
-        gathered = dot(window, counts[chunk])
-        vector = basis[level, :, place]
-        mixed = vector + (PAIR * spread[:, place]) * (gathered[:days] + gathered[days:])
+        window = pl.ds(chunk * CH, 2 * CH)
+        both = jnp.concatenate([scaled[:days, window], scaled[days:, window]], axis=1)
+        gathered = dot(both, jnp.concatenate([counts[chunk], counts[chunk]], axis=0))
+        mixed = basis[level, :, place] + (PAIR * spread[:, place]) * gathered
         day_send[level, 0, :, place] = mixed[:W]
         day_send[level, 1, :, place] = mixed[days - W :]
-        for copy in day_copies(level, chunk):
-            copy.start()
+        basis[level + 1, :, place] = mixed
+
+    def smoothen(level, chunk):
+        place = columns(chunk)
+        mixed = basis[level + 1, :, place]
         high, low = split(mixed)
-        both = dot(toeplitz[...], high)
-        smooth = (DIAG / TAU) * mixed + both[:days] + both[days:] + dot(toeplitz[:days], low)
-        basis[level + 1, :, place] = smooth
-
-    def finish(level, chunk):
+        basis[level + 1, :, place] = (DIAG / TAU) * mixed + dot(
+            toeplitz[...], jnp.concatenate([high, high, low], axis=0)
+        )
+
+    def spatial(level, pair):
+        for group in pair:
+            for chunk in (2 * group, 2 * group + 1):
+                gather(level, chunk)
+        for group in pair:
+            for copy in day_copies(level, group):
+                copy.start()
+        for group in pair:
+            for chunk in (2 * group, 2 * group + 1):
+                smoothen(level, chunk)
+
+    def finish(level, pair):
+        for group in pair:
+            for copy in day_copies(level, group):
+                copy.wait()
+        for group in pair:
+            for chunk in (2 * group, 2 * group + 1):
+                finish_chunk(level, chunk)
+
+    def finish_chunk(level, chunk):
         place = columns(chunk)
-        for copy in day_copies(level, chunk):
-            copy.wait()
-        for side, rows in ((0, slice(0, W)), (1, slice(days - W, days))):
+        smooth = basis[level + 1, :, place]
+        ends = []
+        for side in range(2):
             high, low = split(day_recv[level, side, :, place])
-            both = dot(edge_t[side], high)
-            basis[level + 1, rows, place] = (
-                basis[level + 1, rows, place] + both[:W] + both[W:] + dot(edge_t[side, :W], low)
-            )
+            ends.append(dot(edge_t[side], jnp.concatenate([high, high, low], axis=0)))
+        smooth = jnp.concatenate(
+            [smooth[:W] + ends[0], smooth[W : days - W], smooth[days - W :] + ends[1]], axis=0
+        )
         vector = basis[level, :, place]
-        image = ((noise[:, place] - SHIFT) * (1.0 / TAU)) * vector + mask[:, place].astype(F32) * basis[
-            level + 1, :, place
-        ]
+        image = ((noise[:, place] - SHIFT) * (1.0 / TAU)) * vector + mask[:, place].astype(F32) * smooth
         if level == 1:
             start = basis[0, :, place]
             other = vector - lead[:, :CH] * start
@@ -368,60 +390,45 @@
     def save(level):
         return pltpu.make_async_copy(basis.at[level], basis_out.at[level], store_sem.at[level])
 
-    last = chunks - 1
-    outer = (1, last - 1, 0, last)
-    inner = [c for k in range(2, chunks // 2) for c in (k, last - k)]
-
-    for chunk in outer[:2]:
-        count_chunk(chunk)
-        spatial(0, chunk)
+    groups = chunks // 2
+    inner = tuple(range(1, groups - 1))
+    outer = (0, groups - 1)
+
+    for group in inner:
+        count_chunk(2 * group)
+        count_chunk(2 * group + 1)
+    spatial(0, inner)
     wait_cells(region_copies)
     region_row[:, :L] = jnp.where(has_left, region_recv[0, :1], -1)
     region_row[:, L + tile :] = jnp.where(has_right, region_recv[1, :1], -1)
     column_block(0)
     column_block(1 + tile // L)
+    for group in outer:
+        count_chunk(2 * group)
+        count_chunk(2 * group + 1)
     take_edges(0, copies)
-    for chunk in outer[2:]:
-        count_chunk(chunk)
-        spatial(0, chunk)
-    for chunk in inner:
-        count_chunk(chunk)
-        spatial(0, chunk)
-
-    factor_now = None
+    spatial(0, outer)
+
     for level in range(ITERS - 1):
         if level == 1:
             sums = sums_end(0, 0, 2)
             factor_now = sums[1] / sums[0]
             lead[...] = factor_now
             norm_first = sums[0]
-        for chunk in outer:
-            finish(level, chunk)
+        finish(level, inner)
+        finish(level, outer)
         copies = send_edges(level + 1)
-        for low, high in ((2, 1), (last - 2, last - 1)):
-            finish(level, low)
-            spatial(level + 1, high)
-        take_edges(level + 1, copies)
-        spatial(level + 1, 0)
-        spatial(level + 1, last)
-        rest = inner[2:]
-        for chunk in rest:
-            finish(level, chunk)
         save(level).start()
         if level == 0:
             sums_begin(0, 0, 2)
-        half = len(inner) // 2
-        for chunk in inner[:half]:
-            spatial(level + 1, chunk)
+        spatial(level + 1, inner)
         if level == 0:
             sums_middle(0)
-        for chunk in inner[half:]:
-            spatial(level + 1, chunk)
+        take_edges(level + 1, copies)
+        spatial(level + 1, outer)
     save(ITERS - 1).start()
-    for chunk in outer:
-        finish(ITERS - 1, chunk)
-    for chunk in inner:
-        finish(ITERS - 1, chunk)
+    finish(ITERS - 1, inner)
+    finish(ITERS - 1, outer)
     save(ITERS).start()
     sums_begin(1, 2, 2 * ITERS)
     sums_middle(1)
@@ -450,7 +457,7 @@
     basis, factors = pl.pallas_call(
         functools.partial(kernel, n_cells, n_tm),
         out_shape=(
-            jax.ShapeDtypeStruct((ITERS + 1, days, tile), F32),
+            pltpu.VMEM((ITERS + 1, days, tile), F32),
             jax.ShapeDtypeStruct((8, L), F32),
         ),
         in_specs=[pl.BlockSpec(memory_space=pltpu.SMEM)] + [pl.BlockSpec(memory_space=pl.ANY)] * 2 + [vmem] * 4,
@@ -461,9 +468,9 @@
             pltpu.VMEM((ITERS + 1, days, tile), F32),
             pltpu.VMEM((2 * days, tile + 2 * L), BF16),
             pltpu.VMEM((chunks, 2 * CH, CH), BF16),
-            pltpu.VMEM((2 * days, days), BF16),
-            pltpu.VMEM((2, 2 * W, W), BF16),
-            pltpu.VMEM((tile + 2 * L, L), jnp.int32),
+            pltpu.VMEM((days, 3 * days), BF16),
+            pltpu.VMEM((2, W, 3 * W), BF16),
+            pltpu.VMEM((tile + 2 * L, L), F32),
             pltpu.VMEM((1, tile + 2 * L), jnp.int32),
             pltpu.VMEM((2, 8, L), jnp.int32),
             pltpu.VMEM((2, 8, L), jnp.int32),
@@ -476,8 +483,8 @@
             pltpu.VMEM((2, n_tm, 8, L), F32),
             pltpu.VMEM((2, n_cells, 8, L), F32),
             pltpu.VMEM((1, CH), F32),
-            dma((ITERS, 2, chunks)),
-            dma((ITERS, 2, chunks)),
+            dma((ITERS, 2, chunks // 2)),
+            dma((ITERS, 2, chunks // 2)),
             dma((ITERS, 2)),
             dma((ITERS, 2)),
             dma((2,)),
@@ -490,7 +497,7 @@
             dma((ITERS + 1,)),
         ],
         compiler_params=pltpu.CompilerParams(
-            collective_id=0, has_side_effects=True, vmem_limit_bytes=56 * 1024 * 1024
+            collective_id=0, has_side_effects=True, vmem_limit_bytes=36 * 1024 * 1024
         ),
     )(taps, observed, mask, noise[None, :], spread[None, :], neighbours, regions[None, :])
     rows = 32

time: 54.5 us -> 59.9 us (1.099)
  local copies, waits for them, and re-layouts: 0 us -> 10.6 us
  Pallas kernels: 53.5 us -> 48.2 us
    unnamed x0 -> x18, local copies, waits for them, and re-layouts: none -> 10.6 us
    pallas_call x1, Pallas kernels: 45.8 us -> 40.5 us  [on_device(): pl.pallas_call(functools.partial(kernel, n_cells, n_tm), out_shape=(pltpu...]
where the time goes in v3:
time: 59.9 us; the launch traced here: 59.4 us
  Pallas kernels  48.2 us (80%)
  local copies, waits for them, and re-layouts  10.6 us (18%)
  between operations  0.66 us (1%)
    pallas_call x1, Pallas kernels, on_device(): pl.pallas_call(functools.partial(kernel, n_cells, n_tm), out_shape=(pltpu...  40.5 us
    unnamed x18, local copies, waits for them, and re-layouts  10.6 us
    pallas_call x1, Pallas kernels, on_device(): pl.pallas_call(combine_kernel, grid=(days // rows,), out_shape=(shape, sh...  7.68 us

profile of v3, /device:TPU:0, one launch (start us, length us, event | category | flops | bytes accessed | tf_op | source)
XLA Modules:
  0.0 59.4 jit_solution(12761227077381193121)
XLA Ops:
  0.6 0.0 copy-start.1
  0.6 1.6 %copy-done.1 = f32[256,2048]{1,0:T(8,128)S(1)} copy-done((f32[256,2048]{1,0:T(8,128)S(1)}, f32[256,2048]{1,0:T(8,128)}, u32[]{:S(2)}) %copy-start.1) | copy-done | bytes 2097176
  2.2 0.0 copy-start.2
  2.2 1.6 %copy-done.2 = s32[256,2048]{1,0:T(8,128)S(1)} copy-done((s32[256,2048]{1,0:T(8,128)S(1)}, s32[256,2048]{1,0:T(8,128)}, u32[]{:S(2)}) %copy-start.2) | copy-done | bytes 2097176
  3.8 0.0 copy-start.3
  3.8 0.8 %copy-done.3 = s32[8,2048]{1,0:T(8,128)S(1)} copy-done((s32[8,2048]{1,0:T(8,128)S(1)}, s32[8,2048]{1,0:T(8,128)}, u32[]{:S(2)}) %copy-start.3) | copy-done | bytes 65560
  4.7 0.0 copy-start.4
  4.7 0.7 %copy-done.4 = f32[2048]{0:T(1024)S(1)} copy-done((f32[2048]{0:T(1024)S(1)}, f32[2048]{0:T(1024)}, u32[]{:S(2)}) %copy-start.4) | copy-done | bytes 8216
  5.4 0.0 copy-start.5
  5.4 0.7 %copy-done.5 = f32[2048]{0:T(1024)S(1)} copy-done((f32[2048]{0:T(1024)S(1)}, f32[2048]{0:T(1024)}, u32[]{:S(2)}) %copy-start.5) | copy-done | bytes 8216
  6.1 0.0 copy-start.6
  6.1 0.7 %copy-done.6 = s32[2048]{0:T(1024)S(1)} copy-done((s32[2048]{0:T(1024)S(1)}, s32[2048]{0:T(1024)}, u32[]{:S(2)}) %copy-start.6) | copy-done | bytes 8216
  6.7 0.0 copy-start.8
  6.8 0.7 %copy-done.8 = f32[32]{0:T(128)S(1)} copy-done((f32[32]{0:T(128)S(1)}, f32[32]{0:T(128)}, u32[]{:S(2)}) %copy-start.8) | copy-done | bytes 152
  7.4 40.5 %shard_map.86 = (f32[4,256,2048]{2,1,0:T(8,128)S(1)}, f32[8,128]{1,0:T(8,128)S(1)}) custom-call(f32[32]{0:T(128)S(1)} %copy-done.8, f32[256,2048]{1,0:T(8,128)S(1)} %copy-done.1, s32[256,2048]{1,0:T(8,128)S(1)} %copy-done.2, f32[1,2048]{1,0:T(1,128)S(1)} %bitcast.3, f32[1,2048]{1,0:T(1,128)S(1)} %bitcast.4, s32[8,2048]{1,0:T(8,128)S(1)} %copy-done.3, ...), custom_call_target="tpu_custom_call" | custom-call | tf_op jit(solution)/shard_map/pallas_call | solution.py:457
  47.9 0.0 copy-start
  47.9 3.2 %copy-done = f32[4,256,2048]{2,1,0:T(8,128)} copy-done((f32[4,256,2048]{2,1,0:T(8,128)}, f32[4,256,2048]{2,1,0:T(8,128)S(1)}, u32[]{:S(2)}) %copy-start) | copy-done | bytes 8388632
  51.1 0.0 copy-start.7
  51.1 0.6 copy-done.7
  51.7 7.7 %shard_map.87 = (f32[256,2048]{1,0:T(8,128)}, f32[256,2048]{1,0:T(8,128)}) custom-call(f32[8,128]{1,0:T(8,128)} %copy-done.7, f32[4,256,2048]{2,1,0:T(8,128)} %copy-done), custom_call_target="tpu_custom_call" | custom-call | tf_op jit(solution)/shard_map/pallas_call | solution.py:505
Async XLA Ops:
  0.6 1.6 %copy-start.1 = (f32[256,2048]{1,0:T(8,128)S(1)}, f32[256,2048]{1,0:T(8,128)}, u32[]{:S(2)}) copy-start(f32[256,2048]{1,0:T(8,128)} %observed_hbm.1) | copy-start | bytes 6291460
  2.2 1.6 %copy-start.2 = (s32[256,2048]{1,0:T(8,128)S(1)}, s32[256,2048]{1,0:T(8,128)}, u32[]{:S(2)}) copy-start(s32[256,2048]{1,0:T(8,128)} %mask_hbm.1) | copy-start | bytes 6291460
  3.8 0.8 %copy-start.3 = (s32[8,2048]{1,0:T(8,128)S(1)}, s32[8,2048]{1,0:T(8,128)}, u32[]{:S(2)}) copy-start(s32[8,2048]{1,0:T(8,128)} %neighbours.1) | copy-start | bytes 196612
  4.7 0.7 %copy-start.4 = (f32[2048]{0:T(1024)S(1)}, f32[2048]{0:T(1024)}, u32[]{:S(2)}) copy-start(f32[2048]{0:T(1024)} %param.9) | copy-start | bytes 24580
  5.4 0.7 %copy-start.5 = (f32[2048]{0:T(1024)S(1)}, f32[2048]{0:T(1024)}, u32[]{:S(2)}) copy-start(f32[2048]{0:T(1024)} %param.10) | copy-start | bytes 24580
  6.1 0.7 %copy-start.6 = (s32[2048]{0:T(1024)S(1)}, s32[2048]{0:T(1024)}, u32[]{:S(2)}) copy-start(s32[2048]{0:T(1024)} %param.13) | copy-start | bytes 24580
  6.7 0.7 %copy-start.8 = (f32[32]{0:T(128)S(1)}, f32[32]{0:T(128)}, u32[]{:S(2)}) copy-start(f32[32]{0:T(128)} %taps.1) | copy-start | bytes 388
  47.9 3.2 %copy-start = (f32[4,256,2048]{2,1,0:T(8,128)}, f32[4,256,2048]{2,1,0:T(8,128)S(1)}, u32[]{:S(2)}) copy-start(f32[4,256,2048]{2,1,0:T(8,128)S(1)} %get-tuple-element.5.basis) | copy-start | bytes 25165828
  51.1 0.6 copy-start.7

commit v4 on v3

--- a/solution.py
+++ b/solution.py
@@ -73,8 +73,8 @@
 def kernel(
     n_cells, n_tm,
     taps, observed_hbm, mask_hbm, noise, spread, neighbours, regions,
-    basis_out, factors_out,
-    observed, mask, basis, scaled, counts, toeplitz, edge_t, column_ids, region_row, region_send, region_recv,
+    solution_out, residual_out,
+    observed, mask, last_residual, basis, scaled, counts, toeplitz, edge_t, column_ids, region_row, region_send, region_recv,
     day_send, day_recv, cell_send, cell_recv, partial, moments, gather_tm, gather_cells, lead,
     day_ssem, day_rsem, cell_ssem, cell_rsem, region_ssem, region_rsem,
     tm_ssem, tm_rsem, cells_ssem, cells_rsem, load_sem, store_sem,
@@ -98,12 +98,19 @@
         pl.semaphore_signal(
             barrier, inc=1, device_id={"cells": lax.rem(my_cells + step, n_cells)}, device_id_type=MESH
         )
-    loads = (
-        pltpu.make_async_copy(observed_hbm, observed, load_sem.at[0]),
-        pltpu.make_async_copy(mask_hbm, mask, load_sem.at[1]),
-    )
-    for load in loads:
-        load.start()
+    groups = tile // (2 * CH)
+
+    def loads(group):
+        place = pl.ds(group * 2 * CH, 2 * CH)
+        return (
+            pltpu.make_async_copy(observed_hbm.at[:, place], observed.at[:, place], load_sem.at[0, group]),
+            pltpu.make_async_copy(mask_hbm.at[:, place], mask.at[:, place], load_sem.at[1, group]),
+        )
+
+    order = (0, groups - 1) + tuple(range(1, groups - 1))
+    for group in order:
+        for load in loads(group):
+            load.start()
 
     def to_cells(source, target, ssem, rsem, peer):
         return pltpu.make_async_remote_copy(
@@ -250,16 +257,19 @@
     scaled[:, :L] = jnp.zeros((2 * days, L), BF16)
     scaled[:, L + tile :] = jnp.zeros((2 * days, L), BF16)
 
-    for load in loads:
-        load.wait()
-
-    @pl.loop(0, chunks)
-    def _(chunk):
-        value = observed[:, columns(chunk)] * mask[:, columns(chunk)].astype(F32)
-        basis[0, :, columns(chunk)] = value
-        store_scaled(chunk, value)
-
+    def first_vector(group):
+        for load in loads(group):
+            load.wait()
+        for chunk in (2 * group, 2 * group + 1):
+            value = observed[:, columns(chunk)] * mask[:, columns(chunk)].astype(F32)
+            basis[0, :, columns(chunk)] = value
+            store_scaled(chunk, value)
+
+    first_vector(0)
+    first_vector(groups - 1)
     copies = send_edges(0)
+    for group in order[2:]:
+        first_vector(group)
 
     moments[...] = jnp.zeros_like(moments)
 
@@ -267,16 +277,16 @@
         total = jnp.sum(product.reshape(days // 8, 8, CH), axis=0)
         return total[:, :L] + total[:, L:]
 
-    def day_copies(level, group):
-        place = pl.ds(group * 2 * CH, 2 * CH)
+    def day_copies(level, run):
+        place = pl.ds(run[0] * CH, len(run) * CH)
         return (
             to_tm(
                 day_send.at[level, 0, :, place], day_recv.at[level, 1, :, place],
-                day_ssem.at[level, 0, group], day_rsem.at[level, 1, group], before,
+                day_ssem.at[level, 0, run[0]], day_rsem.at[level, 1, run[0]], before,
             ),
             to_tm(
                 day_send.at[level, 1, :, place], day_recv.at[level, 0, :, place],
-                day_ssem.at[level, 1, group], day_rsem.at[level, 0, group], after,
+                day_ssem.at[level, 1, run[0]], day_rsem.at[level, 0, run[0]], after,
             ),
         )
 
@@ -298,23 +308,23 @@
             toeplitz[...], jnp.concatenate([high, high, low], axis=0)
         )
 
-    def spatial(level, pair):
-        for group in pair:
-            for chunk in (2 * group, 2 * group + 1):
+    def spatial(level, runs):
+        for run in runs:
+            for chunk in run:
                 gather(level, chunk)
-        for group in pair:
-            for copy in day_copies(level, group):
+        for run in runs:
+            for copy in day_copies(level, run):
                 copy.start()
-        for group in pair:
-            for chunk in (2 * group, 2 * group + 1):
+        for run in runs:
+            for chunk in run:
                 smoothen(level, chunk)
 
-    def finish(level, pair):
-        for group in pair:
-            for copy in day_copies(level, group):
+    def finish(level, runs):
+        for run in runs:
+            for copy in day_copies(level, run):
                 copy.wait()
-        for group in pair:
-            for chunk in (2 * group, 2 * group + 1):
+        for run in runs:
+            for chunk in run:
                 finish_chunk(level, chunk)
 
     def finish_chunk(level, chunk):
@@ -387,27 +397,28 @@
             for k in range(first, last)
         ]
 
-    def save(level):
-        return pltpu.make_async_copy(basis.at[level], basis_out.at[level], store_sem.at[level])
-
-    groups = chunks // 2
-    inner = tuple(range(1, groups - 1))
-    outer = (0, groups - 1)
-
-    for group in inner:
-        count_chunk(2 * group)
-        count_chunk(2 * group + 1)
-    spatial(0, inner)
+    half = chunks // 2
+    middle = ((half - 1, half),)
+    rest = (tuple(range(1, half - 1)), tuple(range(half + 1, chunks - 1)))
+    ends = ((0,), (chunks - 1,))
+
+    def count_runs(runs):
+        for run in runs:
+            for chunk in run:
+                count_chunk(chunk)
+
+    count_runs(middle)
+    spatial(0, middle)
+    count_runs(rest)
+    spatial(0, rest)
     wait_cells(region_copies)
     region_row[:, :L] = jnp.where(has_left, region_recv[0, :1], -1)
     region_row[:, L + tile :] = jnp.where(has_right, region_recv[1, :1], -1)
     column_block(0)
     column_block(1 + tile // L)
-    for group in outer:
-        count_chunk(2 * group)
-        count_chunk(2 * group + 1)
+    count_runs(ends)
     take_edges(0, copies)
-    spatial(0, outer)
+    spatial(0, ends)
 
     for level in range(ITERS - 1):
         if level == 1:
@@ -415,37 +426,45 @@
             factor_now = sums[1] / sums[0]
             lead[...] = factor_now
             norm_first = sums[0]
-        finish(level, inner)
-        finish(level, outer)
+        finish(level, middle)
+        finish(level, rest)
+        spatial(level + 1, middle)
+        finish(level, ends)
         copies = send_edges(level + 1)
-        save(level).start()
         if level == 0:
             sums_begin(0, 0, 2)
-        spatial(level + 1, inner)
+        spatial(level + 1, rest)
         if level == 0:
             sums_middle(0)
         take_edges(level + 1, copies)
-        spatial(level + 1, outer)
-    save(ITERS - 1).start()
-    finish(ITERS - 1, inner)
-    finish(ITERS - 1, outer)
-    save(ITERS).start()
+        spatial(level + 1, ends)
+    finish(ITERS - 1, middle)
+    finish(ITERS - 1, rest)
+    finish(ITERS - 1, ends)
     sums_begin(1, 2, 2 * ITERS)
     sums_middle(1)
     rho = SHIFT + TAU * factor_now
     tail = sums_end(1, 2, 2 * ITERS)
     iterate, residual = polynomial_steps([norm_first, jnp.zeros_like(norm_first)] + tail, rho)
-    for k, value in enumerate(iterate + residual):
-        factors_out[pl.ds(k, 1), :] = value[:, :L]
-    factors_out[pl.ds(2 * ITERS + 1, 1), :] = jnp.zeros((1, L), F32)
-    for level in range(ITERS + 1):
-        save(level).wait()
-
-
-def combine_kernel(factors, basis, solution_out, residual_out):
-    levels = [basis[k] for k in range(ITERS + 1)]
-    solution_out[...] = combine([factors[k, 0] for k in range(ITERS)], levels)
-    residual_out[...] = combine([factors[k, 0] for k in range(ITERS, 2 * ITERS + 1)], levels)
+
+    def save(group):
+        place = pl.ds(group * 2 * CH, 2 * CH)
+        return (
+            pltpu.make_async_copy(observed.at[:, place], solution_out.at[:, place], store_sem.at[0, group]),
+            pltpu.make_async_copy(last_residual.at[:, place], residual_out.at[:, place], store_sem.at[1, group]),
+        )
+
+    for group in range(groups):
+        for chunk in (2 * group, 2 * group + 1):
+            place = columns(chunk)
+            levels = [basis[k, :, place] for k in range(ITERS + 1)]
+            observed[:, place] = combine(iterate, levels)
+            last_residual[:, place] = combine(residual, levels)
+        for copy in save(group):
+            copy.start()
+    for group in range(groups):
+        for copy in save(group):
+            copy.wait()
 
 
 def on_device(n_cells, n_tm, observed, mask, noise, spread, taps, neighbours, regions):
@@ -453,18 +472,15 @@
     chunks = tile // CH
     dma = pltpu.SemaphoreType.DMA
     vmem = pl.BlockSpec(memory_space=pltpu.VMEM)
-    shape = jax.ShapeDtypeStruct(observed.shape, F32)
-    basis, factors = pl.pallas_call(
+    return pl.pallas_call(
         functools.partial(kernel, n_cells, n_tm),
-        out_shape=(
-            pltpu.VMEM((ITERS + 1, days, tile), F32),
-            jax.ShapeDtypeStruct((8, L), F32),
-        ),
+        out_shape=(pltpu.VMEM((days, tile), F32), pltpu.VMEM((days, tile), F32)),
         in_specs=[pl.BlockSpec(memory_space=pltpu.SMEM)] + [pl.BlockSpec(memory_space=pl.ANY)] * 2 + [vmem] * 4,
-        out_specs=(pl.BlockSpec(memory_space=pl.ANY), vmem),
+        out_specs=(pl.BlockSpec(memory_space=pl.ANY), pl.BlockSpec(memory_space=pl.ANY)),
         scratch_shapes=[
             pltpu.VMEM((days, tile), F32),
             pltpu.VMEM((days, tile), jnp.int32),
+            pltpu.VMEM((days, tile), F32),
             pltpu.VMEM((ITERS + 1, days, tile), F32),
             pltpu.VMEM((2 * days, tile + 2 * L), BF16),
             pltpu.VMEM((chunks, 2 * CH, CH), BF16),
@@ -483,8 +499,8 @@
             pltpu.VMEM((2, n_tm, 8, L), F32),
             pltpu.VMEM((2, n_cells, 8, L), F32),
             pltpu.VMEM((1, CH), F32),
-            dma((ITERS, 2, chunks // 2)),
-            dma((ITERS, 2, chunks // 2)),
+            dma((ITERS, 2, chunks)),
+            dma((ITERS, 2, chunks)),
             dma((ITERS, 2)),
             dma((ITERS, 2)),
             dma((2,)),
@@ -493,25 +509,13 @@
             dma((2, n_tm)),
             dma((2, n_cells)),
             dma((2, n_cells)),
-            dma((2,)),
-            dma((ITERS + 1,)),
+            dma((2, chunks // 2)),
+            dma((2, chunks // 2)),
         ],
         compiler_params=pltpu.CompilerParams(
-            collective_id=0, has_side_effects=True, vmem_limit_bytes=36 * 1024 * 1024
+            collective_id=0, has_side_effects=True, vmem_limit_bytes=52 * 1024 * 1024
         ),
     )(taps, observed, mask, noise[None, :], spread[None, :], neighbours, regions[None, :])
-    rows = 32
-    block = pl.BlockSpec((rows, tile), lambda i: (i, 0))
-    return pl.pallas_call(
-        combine_kernel,
-        grid=(days // rows,),
-        out_shape=(shape, shape),
-        in_specs=[
-            pl.BlockSpec(memory_space=pltpu.SMEM),
-            pl.BlockSpec((ITERS + 1, rows, tile), lambda i: (0, i, 0)),
-        ],
-        out_specs=(block, block),
-    )(factors, basis)
 
 
 def solution(mesh):

time: 59.9 us -> 43.7 us (0.73)
  local copies, waits for them, and re-layouts: 10.6 us -> 2.64 us
  Pallas kernels: 48.2 us -> 40.3 us
    unnamed x18 -> x2, local copies, waits for them, and re-layouts: 10.6 us -> 2.64 us
    pallas_call x1 -> x0, Pallas kernels: 7.68 us -> none  [on_device(): pl.pallas_call(combine_kernel, grid=(days // rows,), out_shape=(shape, sh...]
where the time goes in v4:
time: 43.7 us; the launch traced here: 43.6 us
  Pallas kernels  40.3 us (92%)
  local copies, waits for them, and re-layouts  2.64 us (6%)
  between operations  0.64 us (1%)
    pallas_call x1, Pallas kernels, on_device(): pl.pallas_call(functools.partial(kernel, n_cells, n_tm), out_shape=(pltpu...  40.3 us
    unnamed x2, local copies, waits for them, and re-layouts  2.64 us

profile of v4, /device:TPU:0, one launch (start us, length us, event | category | flops | bytes accessed | tf_op | source)
XLA Modules:
  0.0 43.6 jit_solution(4954553295530098348)
XLA Ops:
  0.6 40.3 %shard_map.86 = (f32[256,2048]{1,0:T(8,128)S(1)}, f32[256,2048]{1,0:T(8,128)S(1)}) custom-call(f32[32]{0:T(128)} %taps.1, f32[256,2048]{1,0:T(8,128)} %observed_hbm.1, s32[256,2048]{1,0:T(8,128)} %mask_hbm.1, f32[1,2048]{1,0:T(1,128)} %bitcast.3, f32[1,2048]{1,0:T(1,128)} %bitcast.4, s32[8,2048]{1,0:T(8,128)} %neighbours.1, s32[1,2048]{1,0:T(1,128)} %bitcast.5), custom_call_target="tpu_custom_call" | custom-call | tf_op jit(solution)/shard_map/pallas_call | solution.py:475
  40.9 1.3 %copy.11 = f32[256,2048]{1,0:T(8,128)} copy(f32[256,2048]{1,0:T(8,128)S(1)} %get-tuple-element.2) | data formatting | bytes 4194304
  42.3 1.3 %copy.12 = f32[256,2048]{1,0:T(8,128)} copy(f32[256,2048]{1,0:T(8,128)S(1)} %get-tuple-element.3) | data formatting | bytes 4194304

commit v5 on v4

--- a/solution.py
+++ b/solution.py
@@ -77,7 +77,7 @@
     observed, mask, last_residual, basis, scaled, counts, toeplitz, edge_t, column_ids, region_row, region_send, region_recv,
     day_send, day_recv, cell_send, cell_recv, partial, moments, gather_tm, gather_cells, lead,
     day_ssem, day_rsem, cell_ssem, cell_rsem, region_ssem, region_rsem,
-    tm_ssem, tm_rsem, cells_ssem, cells_rsem, load_sem, store_sem,
+    tm_ssem, tm_rsem, cells_ssem, cells_rsem, load_sem, store_sem, gather_all, all_ssem, all_rsem,
 ):
     days, tile = observed.shape
     chunks = tile // CH
@@ -90,13 +90,13 @@
     has_right = my_cells < n_cells - 1
 
     barrier = pltpu.get_barrier_semaphore()
-    for step in range(1, n_tm):
+    peers = [
+        (lax.rem(my_tm + step // n_cells, n_tm), lax.rem(my_cells + step % n_cells, n_cells))
+        for step in range(1, n_tm * n_cells)
+    ]
+    for peer_tm, peer_cells in peers:
         pl.semaphore_signal(
-            barrier, inc=1, device_id={"tm": lax.rem(my_tm + step, n_tm)}, device_id_type=MESH
-        )
-    for step in range(1, n_cells):
-        pl.semaphore_signal(
-            barrier, inc=1, device_id={"cells": lax.rem(my_cells + step, n_cells)}, device_id_type=MESH
+            barrier, inc=1, device_id={"tm": peer_tm, "cells": peer_cells}, device_id_type=MESH
         )
     groups = tile // (2 * CH)
 
@@ -225,34 +225,37 @@
             found = jnp.where(same, found, 0.0)
             counts[chunk, half * L + L - HB : half * L + L - HB + span, half * L : half * L + L] = found.astype(BF16)
 
-    rows_t = 2 * W
-    gap = jnp.abs(
-        lax.broadcasted_iota(jnp.int32, (rows_t, L), 0) + W - lax.broadcasted_iota(jnp.int32, (rows_t, L), 1)
-    )
-    band = jnp.zeros((rows_t, L), F32)
-    for k in range(W):
-        band = jnp.where(gap == k + 1, taps[k] * (TAP_TOTAL / W / TAU), band)
-    wide = jnp.concatenate([band, jnp.zeros((rows_t, days - L), F32)], axis=1)
-    lanes_t = lax.broadcasted_iota(jnp.int32, (rows_t, days), 1)
-    for row in range(0, days, rows_t):
-        shift = (row - W) % days
-        near = pltpu.roll(wide, shift, 1) if shift else wide
-        near = jnp.where((lanes_t >= row - W) & (lanes_t < row + rows_t + W), near, 0.0)
-        high, low = split(near)
-        toeplitz[row : row + rows_t] = jnp.concatenate([high, low, high], axis=1)
-    for side, part in ((0, band[:W, :W]), (1, band[W:, L - W :])):
-        high, low = split(part)
-        edge_t[side] = jnp.concatenate([high, low, high], axis=1)
+    def build_toeplitz():
+        rows_t = 2 * W
+        gap = jnp.abs(
+            lax.broadcasted_iota(jnp.int32, (rows_t, L), 0) + W - lax.broadcasted_iota(jnp.int32, (rows_t, L), 1)
+        )
+        band = jnp.zeros((rows_t, L), F32)
+        for k in range(W):
+            band = jnp.where(gap == k + 1, taps[k] * (TAP_TOTAL / W / TAU), band)
+        wide = jnp.concatenate([band, jnp.zeros((rows_t, days - L), F32)], axis=1)
+        lanes_t = lax.broadcasted_iota(jnp.int32, (rows_t, days), 1)
+        for row in range(0, days, rows_t):
+            shift = (row - W) % days
+            near = pltpu.roll(wide, shift, 1) if shift else wide
+            near = jnp.where((lanes_t >= row - W) & (lanes_t < row + rows_t + W), near, 0.0)
+            high, low = split(near)
+            toeplitz[row : row + rows_t] = jnp.concatenate([high, low, high], axis=1)
+        for side, part in ((0, band[:W, :W]), (1, band[W:, L - W :])):
+            high, low = split(part)
+            edge_t[side] = jnp.concatenate([high, low, high], axis=1)
 
     for block in range(1, 1 + tile // L):
         column_block(block)
 
-    pl.semaphore_wait(barrier, n_tm + n_cells - 2)
-
-    region_send[0] = jnp.broadcast_to(regions[:, :L], (8, L))
-    region_send[1] = jnp.broadcast_to(regions[:, tile - L :], (8, L))
-    region_copies = cell_copies(region_send, region_recv, region_ssem, region_rsem)
-    start_cells(region_copies)
+    middle = (tuple(range(2, chunks - 2)),)
+    rest = ((1,), (chunks - 2,))
+    ends = ((0,), (chunks - 1,))
+
+    def count_runs(runs):
+        for run in runs:
+            for chunk in run:
+                count_chunk(chunk)
 
     scaled[:, :L] = jnp.zeros((2 * days, L), BF16)
     scaled[:, L + tile :] = jnp.zeros((2 * days, L), BF16)
@@ -265,8 +268,14 @@
             basis[0, :, columns(chunk)] = value
             store_scaled(chunk, value)
 
+    count_runs(middle)
     first_vector(0)
     first_vector(groups - 1)
+    pl.semaphore_wait(barrier, n_tm * n_cells - 1)
+    region_send[0] = jnp.broadcast_to(regions[:, :L], (8, L))
+    region_send[1] = jnp.broadcast_to(regions[:, tile - L :], (8, L))
+    region_copies = cell_copies(region_send, region_recv, region_ssem, region_rsem)
+    start_cells(region_copies)
     copies = send_edges(0)
     for group in order[2:]:
         first_vector(group)
@@ -308,13 +317,15 @@
             toeplitz[...], jnp.concatenate([high, high, low], axis=0)
         )
 
-    def spatial(level, runs):
+    def spatial(level, runs, between=None):
         for run in runs:
             for chunk in run:
                 gather(level, chunk)
         for run in runs:
             for copy in day_copies(level, run):
                 copy.start()
+        if between is not None:
+            between()
         for run in runs:
             for chunk in run:
                 smoothen(level, chunk)
@@ -379,36 +390,39 @@
             my_cells, n_cells, to_cells,
         )
 
-    def sums_begin(turn, first, last):
+    def packed_moments(first, last):
         packed = jnp.zeros((8, L), F32)
         for k in range(first, last):
             packed = jnp.where(row_ids == k, jnp.sum(moments[k], axis=0, keepdims=True), packed)
-        partial[turn, 0] = packed
-        start_sum(*over_tm(turn))
-
-    def sums_middle(turn):
-        partial[turn, 1] = end_sum(*over_tm(turn))
-        start_sum(*over_cells(turn))
-
-    def sums_end(turn, first, last):
-        total = end_sum(*over_cells(turn))
+        return packed
+
+    def lane_sums(total, first, last):
         return [
             jnp.broadcast_to(jnp.sum(total[k : k + 1], axis=1, keepdims=True), (1, CH))
             for k in range(first, last)
         ]
 
-    half = chunks // 2
-    middle = ((half - 1, half),)
-    rest = (tuple(range(1, half - 1)), tuple(range(half + 1, chunks - 1)))
-    ends = ((0,), (chunks - 1,))
-
-    def count_runs(runs):
-        for run in runs:
-            for chunk in run:
-                count_chunk(chunk)
-
-    count_runs(middle)
-    spatial(0, middle)
+    mine = my_cells * n_tm + my_tm
+
+    def to_peer(peer_tm, peer_cells, step, slot):
+        return pltpu.make_async_remote_copy(
+            src_ref=gather_all.at[mine], dst_ref=gather_all.at[slot],
+            send_sem=all_ssem.at[step], recv_sem=all_rsem.at[slot],
+            device_id={"tm": peer_tm, "cells": peer_cells}, device_id_type=MESH,
+        )
+
+    def sums_begin(turn, first, last):
+        partial[turn, 0] = packed_moments(first, last)
+        start_sum(*over_tm(turn))
+
+    def sums_middle(turn):
+        partial[turn, 1] = end_sum(*over_tm(turn))
+        start_sum(*over_cells(turn))
+
+    def sums_end(turn, first, last):
+        return lane_sums(end_sum(*over_cells(turn)), first, last)
+
+    spatial(0, middle, build_toeplitz)
     count_runs(rest)
     spatial(0, rest)
     wait_cells(region_copies)
@@ -441,10 +455,16 @@
     finish(ITERS - 1, middle)
     finish(ITERS - 1, rest)
     finish(ITERS - 1, ends)
-    sums_begin(1, 2, 2 * ITERS)
-    sums_middle(1)
+    gather_all[mine] = packed_moments(2, 2 * ITERS)
+    for step, (peer_tm, peer_cells) in enumerate(peers):
+        to_peer(peer_tm, peer_cells, step, mine).start()
     rho = SHIFT + TAU * factor_now
-    tail = sums_end(1, 2, 2 * ITERS)
+    for step, (peer_tm, peer_cells) in enumerate(peers):
+        to_peer(peer_tm, peer_cells, step, peer_cells * n_tm + peer_tm).wait()
+    total = gather_all[0]
+    for index in range(1, n_tm * n_cells):
+        total = total + gather_all[index]
+    tail = lane_sums(total, 2, 2 * ITERS)
     iterate, residual = polynomial_steps([norm_first, jnp.zeros_like(norm_first)] + tail, rho)
 
     def save(group):
@@ -494,10 +514,10 @@
             pltpu.VMEM((ITERS, 2, W, tile), F32),
             pltpu.VMEM((ITERS, 2, days // 4, L), F32),
             pltpu.VMEM((ITERS, 2, days // 4, L), F32),
-            pltpu.VMEM((2, 2, 8, L), F32),
+            pltpu.VMEM((1, 2, 8, L), F32),
             pltpu.VMEM((2 * ITERS, 8, L), F32),
-            pltpu.VMEM((2, n_tm, 8, L), F32),
-            pltpu.VMEM((2, n_cells, 8, L), F32),
+            pltpu.VMEM((1, n_tm, 8, L), F32),
+            pltpu.VMEM((1, n_cells, 8, L), F32),
             pltpu.VMEM((1, CH), F32),
             dma((ITERS, 2, chunks)),
             dma((ITERS, 2, chunks)),
@@ -505,12 +525,15 @@
             dma((ITERS, 2)),
             dma((2,)),
             dma((2,)),
-            dma((2, n_tm)),
-            dma((2, n_tm)),
-            dma((2, n_cells)),
-            dma((2, n_cells)),
+            dma((1, n_tm)),
+            dma((1, n_tm)),
+            dma((1, n_cells)),
+            dma((1, n_cells)),
             dma((2, chunks // 2)),
             dma((2, chunks // 2)),
+            pltpu.VMEM((n_cells * n_tm, 8, L), F32),
+            dma((n_cells * n_tm,)),
+            dma((n_cells * n_tm,)),
         ],
         compiler_params=pltpu.CompilerParams(
             collective_id=0, has_side_effects=True, vmem_limit_bytes=52 * 1024 * 1024

time: 43.7 us -> 44.8 us (1.025)
  Pallas kernels: 40.3 us -> 41.3 us
    pallas_call x1, Pallas kernels: 40.3 us -> 41.3 us  [on_device(): pl.pallas_call(functools.partial(kernel, n_cells, n_tm), out_shape=(pltpu...]
where the time goes in v5:
time: 44.8 us; the launch traced here: 44.6 us
  Pallas kernels  41.3 us (92%)
  local copies, waits for them, and re-layouts  2.64 us (6%)
  between operations  0.64 us (1%)
    pallas_call x1, Pallas kernels, on_device(): pl.pallas_call(functools.partial(kernel, n_cells, n_tm), out_shape=(pltpu...  41.3 us
    unnamed x2, local copies, waits for them, and re-layouts  2.64 us

profile of v5, /device:TPU:0, one launch (start us, length us, event | category | flops | bytes accessed | tf_op | source)
XLA Modules:
  0.0 44.6 jit_solution(861497599024206099)
XLA Ops:
  0.6 41.3 %shard_map.86 = (f32[256,2048]{1,0:T(8,128)S(1)}, f32[256,2048]{1,0:T(8,128)S(1)}) custom-call(f32[32]{0:T(128)} %taps.1, f32[256,2048]{1,0:T(8,128)} %observed_hbm.1, s32[256,2048]{1,0:T(8,128)} %mask_hbm.1, f32[1,2048]{1,0:T(1,128)} %bitcast.3, f32[1,2048]{1,0:T(1,128)} %bitcast.4, s32[8,2048]{1,0:T(8,128)} %neighbours.1, s32[1,2048]{1,0:T(1,128)} %bitcast.5), custom_call_target="tpu_custom_call" | custom-call | tf_op jit(solution)/shard_map/pallas_call | solution.py:495
  42.0 1.3 %copy.11 = f32[256,2048]{1,0:T(8,128)} copy(f32[256,2048]{1,0:T(8,128)S(1)} %get-tuple-element.2) | data formatting | bytes 4194304
  43.3 1.3 %copy.12 = f32[256,2048]{1,0:T(8,128)} copy(f32[256,2048]{1,0:T(8,128)S(1)} %get-tuple-element.3) | data formatting | bytes 4194304

commit v6 on v5

--- a/solution.py
+++ b/solution.py
@@ -77,7 +77,7 @@
     observed, mask, last_residual, basis, scaled, counts, toeplitz, edge_t, column_ids, region_row, region_send, region_recv,
     day_send, day_recv, cell_send, cell_recv, partial, moments, gather_tm, gather_cells, lead,
     day_ssem, day_rsem, cell_ssem, cell_rsem, region_ssem, region_rsem,
-    tm_ssem, tm_rsem, cells_ssem, cells_rsem, load_sem, store_sem, gather_all, all_ssem, all_rsem,
+    tm_ssem, tm_rsem, cells_ssem, cells_rsem, load_sem, store_sem,
 ):
     days, tile = observed.shape
     chunks = tile // CH
@@ -90,13 +90,13 @@
     has_right = my_cells < n_cells - 1
 
     barrier = pltpu.get_barrier_semaphore()
-    peers = [
-        (lax.rem(my_tm + step // n_cells, n_tm), lax.rem(my_cells + step % n_cells, n_cells))
-        for step in range(1, n_tm * n_cells)
-    ]
-    for peer_tm, peer_cells in peers:
+    for step in range(1, n_tm):
         pl.semaphore_signal(
-            barrier, inc=1, device_id={"tm": peer_tm, "cells": peer_cells}, device_id_type=MESH
+            barrier, inc=1, device_id={"tm": lax.rem(my_tm + step, n_tm)}, device_id_type=MESH
+        )
+    for step in range(1, n_cells):
+        pl.semaphore_signal(
+            barrier, inc=1, device_id={"cells": lax.rem(my_cells + step, n_cells)}, device_id_type=MESH
         )
     groups = tile // (2 * CH)
 
@@ -248,7 +248,7 @@
     for block in range(1, 1 + tile // L):
         column_block(block)
 
-    middle = (tuple(range(2, chunks - 2)),)
+    middle = (tuple(range(3, chunks - 3)), (2,), (chunks - 3,))
     rest = ((1,), (chunks - 2,))
     ends = ((0,), (chunks - 1,))
 
@@ -271,7 +271,7 @@
     count_runs(middle)
     first_vector(0)
     first_vector(groups - 1)
-    pl.semaphore_wait(barrier, n_tm * n_cells - 1)
+    pl.semaphore_wait(barrier, n_tm + n_cells - 2)
     region_send[0] = jnp.broadcast_to(regions[:, :L], (8, L))
     region_send[1] = jnp.broadcast_to(regions[:, tile - L :], (8, L))
     region_copies = cell_copies(region_send, region_recv, region_ssem, region_rsem)
@@ -402,15 +402,6 @@
             for k in range(first, last)
         ]
 
-    mine = my_cells * n_tm + my_tm
-
-    def to_peer(peer_tm, peer_cells, step, slot):
-        return pltpu.make_async_remote_copy(
-            src_ref=gather_all.at[mine], dst_ref=gather_all.at[slot],
-            send_sem=all_ssem.at[step], recv_sem=all_rsem.at[slot],
-            device_id={"tm": peer_tm, "cells": peer_cells}, device_id_type=MESH,
-        )
-
     def sums_begin(turn, first, last):
         partial[turn, 0] = packed_moments(first, last)
         start_sum(*over_tm(turn))
@@ -422,7 +413,8 @@
     def sums_end(turn, first, last):
         return lane_sums(end_sum(*over_cells(turn)), first, last)
 
-    spatial(0, middle, build_toeplitz)
+    spatial(0, middle[:1], build_toeplitz)
+    spatial(0, middle[1:])
     count_runs(rest)
     spatial(0, rest)
     wait_cells(region_copies)
@@ -455,16 +447,10 @@
     finish(ITERS - 1, middle)
     finish(ITERS - 1, rest)
     finish(ITERS - 1, ends)
-    gather_all[mine] = packed_moments(2, 2 * ITERS)
-    for step, (peer_tm, peer_cells) in enumerate(peers):
-        to_peer(peer_tm, peer_cells, step, mine).start()
+    sums_begin(1, 2, 2 * ITERS)
+    sums_middle(1)
     rho = SHIFT + TAU * factor_now
-    for step, (peer_tm, peer_cells) in enumerate(peers):
-        to_peer(peer_tm, peer_cells, step, peer_cells * n_tm + peer_tm).wait()
-    total = gather_all[0]
-    for index in range(1, n_tm * n_cells):
-        total = total + gather_all[index]
-    tail = lane_sums(total, 2, 2 * ITERS)
+    tail = sums_end(1, 2, 2 * ITERS)
     iterate, residual = polynomial_steps([norm_first, jnp.zeros_like(norm_first)] + tail, rho)
 
     def save(group):
@@ -514,10 +500,10 @@
             pltpu.VMEM((ITERS, 2, W, tile), F32),
             pltpu.VMEM((ITERS, 2, days // 4, L), F32),
             pltpu.VMEM((ITERS, 2, days // 4, L), F32),
-            pltpu.VMEM((1, 2, 8, L), F32),
+            pltpu.VMEM((2, 2, 8, L), F32),
             pltpu.VMEM((2 * ITERS, 8, L), F32),
-            pltpu.VMEM((1, n_tm, 8, L), F32),
-            pltpu.VMEM((1, n_cells, 8, L), F32),
+            pltpu.VMEM((2, n_tm, 8, L), F32),
+            pltpu.VMEM((2, n_cells, 8, L), F32),
             pltpu.VMEM((1, CH), F32),
             dma((ITERS, 2, chunks)),
             dma((ITERS, 2, chunks)),
@@ -525,15 +511,12 @@
             dma((ITERS, 2)),
             dma((2,)),
             dma((2,)),
-            dma((1, n_tm)),
-            dma((1, n_tm)),
-            dma((1, n_cells)),
-            dma((1, n_cells)),
+            dma((2, n_tm)),
+            dma((2, n_tm)),
+            dma((2, n_cells)),
+            dma((2, n_cells)),
             dma((2, chunks // 2)),
             dma((2, chunks // 2)),
-            pltpu.VMEM((n_cells * n_tm, 8, L), F32),
-            dma((n_cells * n_tm,)),
-            dma((n_cells * n_tm,)),
         ],
         compiler_params=pltpu.CompilerParams(
             collective_id=0, has_side_effects=True, vmem_limit_bytes=52 * 1024 * 1024

time: 44.8 us -> 44.9 us (level)
  no operation moved by 1% of the time
where the time goes in v6:
time: 44.9 us; the launch traced here: 44.7 us
  Pallas kernels  41.4 us (92%)
  local copies, waits for them, and re-layouts  2.64 us (6%)
  between operations  0.64 us (1%)
    pallas_call x1, Pallas kernels, on_device(): pl.pallas_call(functools.partial(kernel, n_cells, n_tm), out_shape=(pltpu...  41.4 us
    unnamed x2, local copies, waits for them, and re-layouts  2.64 us

profile of v6, /device:TPU:0, one launch (start us, length us, event | category | flops | bytes accessed | tf_op | source)
XLA Modules:
  0.0 44.7 jit_solution(12211265152055107588)
XLA Ops:
  0.6 41.4 %shard_map.86 = (f32[256,2048]{1,0:T(8,128)S(1)}, f32[256,2048]{1,0:T(8,128)S(1)}) custom-call(f32[32]{0:T(128)} %taps.1, f32[256,2048]{1,0:T(8,128)} %observed_hbm.1, s32[256,2048]{1,0:T(8,128)} %mask_hbm.1, f32[1,2048]{1,0:T(1,128)} %bitcast.3, f32[1,2048]{1,0:T(1,128)} %bitcast.4, s32[8,2048]{1,0:T(8,128)} %neighbours.1, s32[1,2048]{1,0:T(1,128)} %bitcast.5), custom_call_target="tpu_custom_call" | custom-call | tf_op jit(solution)/shard_map/pallas_call | solution.py:481
  42.1 1.3 %copy.11 = f32[256,2048]{1,0:T(8,128)} copy(f32[256,2048]{1,0:T(8,128)S(1)} %get-tuple-element.2) | data formatting | bytes 4194304
  43.4 1.3 %copy.12 = f32[256,2048]{1,0:T(8,128)} copy(f32[256,2048]{1,0:T(8,128)S(1)} %get-tuple-element.3) | data formatting | bytes 4194304
